TPU v7x, 256 devices: a whole 4x4x8 slice. The times are simulated.
256 devices in a mesh: cells: 16 (over y_hi, z), modes: 16 (over y_lo, x, core).
Axes of the slice: x: 4, y: 4 (y_hi: 2, y_lo: 2; y = y_hi * 2 + y_lo), z: 8, core: 2. Of those that a mesh axis runs over, the one named last changes fastest.
Arguments:
- theta: float32 [8192, 32], P('modes'), may hold values from -6 to 6
- basis: bfloat16 [32768, 8192], P('cells', 'modes'), may hold values from -0.0625 to 0.0625
- mean_logk: float32 [32768], P('cells'), may hold values from -3 to 3
- face_mult: float32 [3, 32768], P(None, 'cells'), may hold values from 0.3 to 3
- storage: float32 [32768], P('cells'), may hold values from 0.05 to 0.5
- sources: float32 [32768], P('cells'), may hold values from -6 to 6
- obs_data: float32 [32768], P('cells'), may hold values from -6 to 6
- obs_weight: float32 [32768], P('cells'), may hold values from 0.1 to 1
- fault_pairs: int32 [4096, 2], P('cells'), may hold values from 0 to 2047, as said below
- fault_mult: float32 [4096], P('cells'), may hold values from 0.1 to 1
- noise: float32 [8192, 32], P('modes'), may hold values from -6 to 6
Outputs:
- theta_next: float32 [8192, 32], P('modes')
- grad: float32 [8192, 32], P('modes')
- pressure: float32 [32, 32768], P('modes', 'cells')
Inputs may be any that keep to these rules, and one draw needn't show every extreme that they name: `fault_pairs`: each block of 256 slots lists its live connections first; each joins a cell (x, y, z) of the block with (x, y+1, z+s), 1 <= s <= 3; the remaining slots pair a cell with itself. Some block is full in every draw.
All inputs are finite; a program needn't handle non-finite values.
Results may differ from a plain program's by a relative error of at most 0.0047.
Values may be sent and summed in bfloat16 or wider, within the bound.
No kernel may reach another device: no remote copies, remote signals or barrier semaphores. Data moves between devices by JAX's collectives and lax.ppermute only.
A program may use at most 64 MiB of HBM per device.

v0:
```python
import math

import jax
import jax.numpy as jnp
from jax import lax
from jax.sharding import PartitionSpec as P

NY = 32
NZ = 64
SWEEPS = 6


LOW_EIG = 0.1
HIGH_EIG = 1.9
STEP_SIZE = 0.01


def extended(block, sides, width):
    for axis, dim in sides:
        count = lax.axis_size(axis)
        forward = [(i, i + 1) for i in range(count - 1)]
        backward = [(target, source) for source, target in forward]
        low = lax.ppermute(
            lax.slice_in_dim(block, block.shape[dim] - width, None, axis=dim), axis, forward
        )
        high = lax.ppermute(lax.slice_in_dim(block, 0, width, axis=dim), axis, backward)
        block = jnp.concatenate([low, block, high], axis=dim)
    return block


def harmonic(left, right):
    return 2.0 * left * right / (left + right)


def pad_axis(array, axis, before, after):
    widths = [(0, 0)] * array.ndim
    widths[axis] = (before, after)
    return jnp.pad(array, widths)


def transmit(perm_ext, mult_ext, mult_y, mult_z, near_cell, far_cell, fault_mult, depth_y, depth_z):
    chains_n = perm_ext.shape[0]
    layers = perm_ext.shape[1] - 2
    trans_x = harmonic(perm_ext[:, :-1], perm_ext[:, 1:]) * mult_ext[:, :-1]
    perm = perm_ext[:, 1:-1].reshape(chains_n, layers, depth_y, depth_z)
    trans_y = (
        harmonic(perm[:, :, :-1], perm[:, :, 1:])
        * mult_y.reshape(1, layers, depth_y, depth_z)[:, :, :-1]
    )
    trans_z = (
        harmonic(perm[..., :-1], perm[..., 1:])
        * mult_z.reshape(1, layers, depth_y, depth_z)[..., :-1]
    )
    flat = perm.reshape(chains_n, -1)
    live = fault_mult * (near_cell != far_cell).astype(jnp.float32)
    trans_n = harmonic(flat[:, near_cell], flat[:, far_cell]) * live[None]
    return (trans_x, trans_y, trans_z, trans_n)


def diagonal_of(trans, storage, near_cell, far_cell, depth_y, depth_z):
    trans_x, trans_y, trans_z, trans_n = trans
    chains_n = trans_x.shape[0]
    layers = trans_x.shape[1] - 1
    total = (trans_x[:, 1:] + trans_x[:, :-1]).reshape(chains_n, layers, depth_y, depth_z)
    total = total + pad_axis(trans_y, 2, 0, 1) + pad_axis(trans_y, 2, 1, 0)
    total = total + pad_axis(trans_z, 3, 0, 1) + pad_axis(trans_z, 3, 1, 0)
    total = total.reshape(chains_n, -1)
    total = total.at[:, near_cell].add(trans_n).at[:, far_cell].add(trans_n)
    return total + storage[None]


def operate(field_ext, trans, storage, near_cell, far_cell, depth_y, depth_z):
    trans_x, trans_y, trans_z, trans_n = trans
    chains_n = field_ext.shape[0]
    layers = field_ext.shape[1] - 2
    flux_x = trans_x * (field_ext[:, :-1] - field_ext[:, 1:])
    result = (flux_x[:, 1:] - flux_x[:, :-1]).reshape(chains_n, layers, depth_y, depth_z)
    field = field_ext[:, 1:-1].reshape(chains_n, layers, depth_y, depth_z)
    flux_y = trans_y * (field[:, :, :-1] - field[:, :, 1:])
    result = result + pad_axis(flux_y, 2, 0, 1) - pad_axis(flux_y, 2, 1, 0)
    flux_z = trans_z * (field[..., :-1] - field[..., 1:])
    result = result + pad_axis(flux_z, 3, 0, 1) - pad_axis(flux_z, 3, 1, 0)
    result = result.reshape(chains_n, -1)
    flat = field.reshape(chains_n, -1)
    flux_n = trans_n * (flat[:, near_cell] - flat[:, far_cell])
    result = result.at[:, near_cell].add(flux_n).at[:, far_cell].add(-flux_n)
    return result + storage[None] * flat


def solve(rhs, apply_fn, diag):
    center = 0.5 * (HIGH_EIG + LOW_EIG)
    half = 0.5 * (HIGH_EIG - LOW_EIG)
    sigma = center / half
    resid = rhs / diag
    direction = resid / center
    iterate = jnp.zeros_like(rhs)
    rho = jnp.asarray(1.0 / sigma, dtype=rhs.dtype)

    def sweep_step(sweep, carry):
        iterate, resid, direction, rho = carry
        iterate = iterate + direction
        resid = resid - apply_fn(direction) / diag
        rho_next = 1.0 / (2.0 * sigma - rho)
        direction = rho_next * rho * direction + 2.0 * rho_next / half * resid
        return (iterate, resid, direction, rho_next)

    iterate, resid, direction, rho = lax.fori_loop(
        0, SWEEPS, sweep_step, (iterate, resid, direction, rho)
    )
    return iterate + direction


def gradient_of(pres_ext, adj_ext, perm_ext, trans, near_cell, far_cell, depth_y, depth_z):
    trans_x, trans_y, trans_z, trans_n = trans
    chains_n = perm_ext.shape[0]
    layers = perm_ext.shape[1] - 2
    coef_x = (
        -(adj_ext[:, :-1] - adj_ext[:, 1:])
        * (pres_ext[:, :-1] - pres_ext[:, 1:])
        * trans_x
        / (perm_ext[:, :-1] + perm_ext[:, 1:])
    )
    result = coef_x[:, 1:] * perm_ext[:, 2:] + coef_x[:, :-1] * perm_ext[:, :-2]
    result = result.reshape(chains_n, layers, depth_y, depth_z)
    shape4 = (chains_n, layers, depth_y, depth_z)
    perm = perm_ext[:, 1:-1].reshape(shape4)
    pres = pres_ext[:, 1:-1].reshape(shape4)
    adj = adj_ext[:, 1:-1].reshape(shape4)
    coef_y = (
        -(adj[:, :, :-1] - adj[:, :, 1:])
        * (pres[:, :, :-1] - pres[:, :, 1:])
        * trans_y
        / (perm[:, :, :-1] + perm[:, :, 1:])
    )
    result = (
        result
        + pad_axis(coef_y * perm[:, :, 1:], 2, 0, 1)
        + pad_axis(coef_y * perm[:, :, :-1], 2, 1, 0)
    )
    coef_z = (
        -(adj[..., :-1] - adj[..., 1:])
        * (pres[..., :-1] - pres[..., 1:])
        * trans_z
        / (perm[..., :-1] + perm[..., 1:])
    )
    result = (
        result
        + pad_axis(coef_z * perm[..., 1:], 3, 0, 1)
        + pad_axis(coef_z * perm[..., :-1], 3, 1, 0)
    )
    result = result.reshape(chains_n, -1)
    perm_f = perm.reshape(chains_n, -1)
    pres_f = pres.reshape(chains_n, -1)
    adj_f = adj.reshape(chains_n, -1)
    perm_a = perm_f[:, near_cell]
    perm_b = perm_f[:, far_cell]
    coef_n = (
        -(adj_f[:, near_cell] - adj_f[:, far_cell])
        * (pres_f[:, near_cell] - pres_f[:, far_cell])
        * trans_n
        / (perm_a + perm_b)
    )
    return result.at[:, near_cell].add(coef_n * perm_b).at[:, far_cell].add(coef_n * perm_a)


def physics(logk, face_mult, storage, sources, obs_data, obs_weight, fault_pairs, fault_mult):
    chains_n, cells_n = logk.shape
    faces = NY * NZ
    layers = cells_n // faces
    near_cell = fault_pairs[:, 0]
    far_cell = fault_pairs[:, 1]
    perm = jnp.exp(logk).reshape(chains_n, layers, faces)
    stacked = jnp.concatenate([perm, face_mult[0].reshape(1, layers, faces)], 0)
    stacked_ext = extended(stacked, (("cells", 1),), 1)
    perm_ext = stacked_ext[:chains_n]
    mult_ext = stacked_ext[chains_n:]
    trans = transmit(
        perm_ext, mult_ext, face_mult[1], face_mult[2], near_cell, far_cell, fault_mult, NY, NZ
    )
    diag = diagonal_of(trans, storage, near_cell, far_cell, NY, NZ)

    def apply_fn(field):
        field_ext = extended(field.reshape(chains_n, layers, faces), (("cells", 1),), 1)
        return operate(field_ext, trans, storage, near_cell, far_cell, NY, NZ)

    rhs = jnp.broadcast_to(sources[None], (chains_n, cells_n))
    pressure = solve(rhs, apply_fn, diag)
    misfit = obs_weight[None] * (pressure - obs_data[None])
    adjoint = solve(misfit, apply_fn, diag)
    both = jnp.concatenate([pressure, adjoint], 0).reshape(2 * chains_n, layers, faces)
    both_ext = extended(both, (("cells", 1),), 1)
    glogk = gradient_of(
        both_ext[:chains_n], both_ext[chains_n:], perm_ext, trans, near_cell, far_cell, NY, NZ
    )
    return (pressure, glogk)


def body(
    theta,
    basis,
    mean_logk,
    face_mult,
    storage,
    sources,
    obs_data,
    obs_weight,
    fault_pairs,
    fault_mult,
    noise,
):
    chains = theta.shape[1]
    share = chains // lax.axis_size("modes")
    theta_b = theta.astype(jnp.bfloat16)
    local_field = lax.dot_general(
        theta_b, basis, (((0,), (1,)), ((), ())), preferred_element_type=jnp.float32
    )
    partial_field = lax.psum(local_field, "modes")
    logk = mean_logk[None] + partial_field
    pressure, glogk = physics(
        logk, face_mult, storage, sources, obs_data, obs_weight, fault_pairs, fault_mult
    )
    glogk_b = glogk.astype(jnp.bfloat16)
    grad_rows = jnp.dot(glogk_b, basis, preferred_element_type=jnp.float32)
    pressure_out = lax.dynamic_slice_in_dim(pressure, lax.axis_index("modes") * share, share, 0)
    mode_grad = lax.psum(grad_rows, "cells")
    grad = mode_grad.T
    theta_next = theta - STEP_SIZE * (grad + theta) + math.sqrt(2.0 * STEP_SIZE) * noise
    return (theta_next, grad, pressure_out)


def solution(mesh):
    return jax.shard_map(
        body,
        mesh=mesh,
        in_specs=(
            P("modes", None),
            P("cells", "modes"),
            P("cells"),
            P(None, "cells"),
            P("cells"),
            P("cells"),
            P("cells"),
            P("cells"),
            P("cells", None),
            P("cells"),
            P("modes", None),
        ),
        out_specs=(P("modes", None), P("modes", None), P("modes", "cells")),
        check_vma=False,
    )
```

profile of v0, /device:TPU:8, one launch (start us, length us, event | category | flops | bytes accessed | tf_op | source)
XLA Modules:
  0.0 856.6 jit_solution(11891560103931221962)
XLA Ops:
  12.6 122.7 %all-reduce.19.cloned.1.call-done = f32[32,2048]{1,0:T(8,128)} async-done(((f32[32,2048]{1,0:T(8,128)}), f32[32,2048]{1,0:T(8,128)}) %all-reduce.19.cloned.1.call-update) | async-done | bytes 262160 | tf_op jit(solution)/shard_map/psum | solution.py:217
  137.1 4.2 collective-permute-start.4
  168.0 218.8 %while.38 = (s32[]{:T(128)}, f32[32,2048]{0,1:T(8,128)}, f32[32,2048]{0,1:T(8,128)}, f32[32,2048]{0,1:T(8,128)S(1)}, f32[]{:T(128)}, /*index=5*/f32[32,2,2048]{2...) while((s32[]{:T(128)}, f32[32,2048]{0,1:T(8,128)}, ...), condition=%wide.region_6.7_spmd.clone, body=%wide.region_3.6_spmd.clone.sunk | while | flops 1758727 | bytes 15995359 | solution.py:107
  168.3 5.3 collective-permute-start
  204.5 5.3 collective-permute-start
  236.5 4.2 multiply_add_fusion.5
  241.0 5.3 collective-permute-start
  273.0 4.2 multiply_add_fusion.5
  277.5 5.3 collective-permute-start
  309.5 4.2 multiply_add_fusion.5
  314.1 5.3 collective-permute-start
  346.0 4.2 multiply_add_fusion.5
  350.6 5.3 collective-permute-start
  382.6 4.2 multiply_add_fusion.5
  394.5 223.6 %while.39 = (s32[]{:T(128)}, f32[32,2048]{0,1:T(8,128)}, f32[32,2048]{0,1:T(8,128)}, f32[32,2048]{0,1:T(8,128)S(1)}, f32[]{:T(128)}, /*index=5*/f32[32,2,2048]{2...) while((s32[]{:T(128)}, f32[32,2048]{0,1:T(8,128)}, ...), condition=%wide.region_10.11_spmd.clone, body=%wide.region_7.10_spmd.clone.sunk | while | flops 1758727 | bytes 15995359 | solution.py:107
  394.8 5.3 collective-permute-start.2
  422.7 4.1 scatter_custom_fusion.35
  431.0 5.5 collective-permute-start.2
  463.2 4.2 multiply_add_fusion.6
  467.8 5.8 collective-permute-start.2
  500.2 4.2 multiply_add_fusion.6
  504.8 5.8 collective-permute-start.2
  537.3 4.2 multiply_add_fusion.6
  541.8 5.9 collective-permute-start.2
  574.4 4.2 multiply_add_fusion.6
  579.0 8.2 collective-permute-start.2
  613.9 4.2 multiply_add_fusion.6
  637.2 7.5 collective-permute-start.6
  654.6 4.7 collective-permute-done.7
  668.6 4.4 scatter_custom_fusion.6
  673.0 4.4 scatter_custom_fusion.7
  680.4 166.4 %all-reduce.21.cloned.1.call-done = f32[512,32]{0,1:T(8,128)} async-done(((f32[512,32]{0,1:T(8,128)}), f32[512,32]{0,1:T(8,128)}) %all-reduce.21.cloned.1.call-update) | async-done | bytes 65552 | tf_op jit(solution)/shard_map/psum | solution.py:225
  (540 shorter events, 411.9 us)
Async XLA Ops:
  7.2 128.1 %all-reduce.19.cloned.1.call-start = ((), (), s32[]{:S(2)}) async-start(), calls=%async_computation | async-start | bytes 524288 | tf_op jit(solution)/shard_map/psum | solution.py:217
  11.1 835.7 %all-reduce.21.cloned.1.call-start = ((), (), s32[]{:S(2)}) async-start(), calls=%async_computation.1 | async-start | bytes 131072 | tf_op jit(solution)/shard_map/psum | solution.py:225
  137.1 15.4 %collective-permute-start.4 = (f32[33,1,2048]{2,0,1:T(8,128)}, f32[33,1,2048]{2,0,1:T(8,128)}, u32[]{:S(2)}, u32[]{:S(2)}) collective-permute-start(f32[33,1,2048]{2,0,1:T(8,128)} %pad_maximum_fusion.4), channel_id=1, source_target_pairs={{0,16},{16,32},{32,48},{48,64},{64,80},{80,96},{96,112},{112,128},... | collective-permute-start | bytes 811016 | tf_op jit(solution)/shard_map/ppermute | solution.py:23
  141.3 13.1 %collective-permute-start.5 = (f32[33,1,2048]{2,0,1:T(8,128)}, f32[33,1,2048]{2,0,1:T(8,128)}, u32[]{:S(2)}, u32[]{:S(2)}) collective-permute-start(f32[33,1,2048]{2,0,1:T(8,128)} %pad_maximum_fusion.4), channel_id=1, source_target_pairs={{16,0},{32,16},{48,32},{64,48},{80,64},{96,80},{112,96},{128,112},... | collective-permute-start | bytes 811016 | tf_op jit(solution)/shard_map/ppermute | solution.py:26
  168.3 16.9 %collective-permute-start = (f32[32,1,2048]{2,0,1:T(8,128)S(1)}, f32[32,1,2048]{2,0,1:T(8,128)}, u32[]{:S(2)}, u32[]{:S(2)}) collective-permute-start(f32[32,1,2048]{2,0,1:T(8,128)S(1)} %bitcast.182), channel_id=1, source_target_pairs={{0,16},{16,32},{32,48},{48,64},{64,80},{80,96},{96,112},{112,128},... | collective-permute-start | bytes 786440 | tf_op jit(solution)/shard_map/while/body/eval_jaxpr/ppermute | solution.py:23
  173.6 11.6 %collective-permute-start.1 = (f32[32,1,2048]{2,0,1:T(8,128)S(1)}, f32[32,1,2048]{2,0,1:T(8,128)}, u32[]{:S(2)}, u32[]{:S(2)}) collective-permute-start(f32[32,1,2048]{2,0,1:T(8,128)S(1)} %bitcast.183), channel_id=1, source_target_pairs={{16,0},{32,16},{48,32},{64,48},{80,64},{96,80},{112,96},{128,112},... | collective-permute-start | bytes 786440 | tf_op jit(solution)/shard_map/while/body/eval_jaxpr/ppermute | solution.py:26
  204.5 16.9 %collective-permute-start = (f32[32,1,2048]{2,0,1:T(8,128)S(1)}, f32[32,1,2048]{2,0,1:T(8,128)}, u32[]{:S(2)}, u32[]{:S(2)}) collective-permute-start(f32[32,1,2048]{2,0,1:T(8,128)S(1)} %bitcast.182), channel_id=1, source_target_pairs={{0,16},{16,32},{32,48},{48,64},{64,80},{80,96},{96,112},{112,128},... | collective-permute-start | bytes 786440 | tf_op jit(solution)/shard_map/while/body/eval_jaxpr/ppermute | solution.py:23
  209.8 11.6 %collective-permute-start.1 = (f32[32,1,2048]{2,0,1:T(8,128)S(1)}, f32[32,1,2048]{2,0,1:T(8,128)}, u32[]{:S(2)}, u32[]{:S(2)}) collective-permute-start(f32[32,1,2048]{2,0,1:T(8,128)S(1)} %bitcast.183), channel_id=1, source_target_pairs={{16,0},{32,16},{48,32},{64,48},{80,64},{96,80},{112,96},{128,112},... | collective-permute-start | bytes 786440 | tf_op jit(solution)/shard_map/while/body/eval_jaxpr/ppermute | solution.py:26
  241.0 16.9 %collective-permute-start = (f32[32,1,2048]{2,0,1:T(8,128)S(1)}, f32[32,1,2048]{2,0,1:T(8,128)}, u32[]{:S(2)}, u32[]{:S(2)}) collective-permute-start(f32[32,1,2048]{2,0,1:T(8,128)S(1)} %bitcast.182), channel_id=1, source_target_pairs={{0,16},{16,32},{32,48},{48,64},{64,80},{80,96},{96,112},{112,128},... | collective-permute-start | bytes 786440 | tf_op jit(solution)/shard_map/while/body/eval_jaxpr/ppermute | solution.py:23
  246.3 11.6 %collective-permute-start.1 = (f32[32,1,2048]{2,0,1:T(8,128)S(1)}, f32[32,1,2048]{2,0,1:T(8,128)}, u32[]{:S(2)}, u32[]{:S(2)}) collective-permute-start(f32[32,1,2048]{2,0,1:T(8,128)S(1)} %bitcast.183), channel_id=1, source_target_pairs={{16,0},{32,16},{48,32},{64,48},{80,64},{96,80},{112,96},{128,112},... | collective-permute-start | bytes 786440 | tf_op jit(solution)/shard_map/while/body/eval_jaxpr/ppermute | solution.py:26
  277.5 16.9 %collective-permute-start = (f32[32,1,2048]{2,0,1:T(8,128)S(1)}, f32[32,1,2048]{2,0,1:T(8,128)}, u32[]{:S(2)}, u32[]{:S(2)}) collective-permute-start(f32[32,1,2048]{2,0,1:T(8,128)S(1)} %bitcast.182), channel_id=1, source_target_pairs={{0,16},{16,32},{32,48},{48,64},{64,80},{80,96},{96,112},{112,128},... | collective-permute-start | bytes 786440 | tf_op jit(solution)/shard_map/while/body/eval_jaxpr/ppermute | solution.py:23
  282.8 11.6 %collective-permute-start.1 = (f32[32,1,2048]{2,0,1:T(8,128)S(1)}, f32[32,1,2048]{2,0,1:T(8,128)}, u32[]{:S(2)}, u32[]{:S(2)}) collective-permute-start(f32[32,1,2048]{2,0,1:T(8,128)S(1)} %bitcast.183), channel_id=1, source_target_pairs={{16,0},{32,16},{48,32},{64,48},{80,64},{96,80},{112,96},{128,112},... | collective-permute-start | bytes 786440 | tf_op jit(solution)/shard_map/while/body/eval_jaxpr/ppermute | solution.py:26
  314.1 16.9 %collective-permute-start = (f32[32,1,2048]{2,0,1:T(8,128)S(1)}, f32[32,1,2048]{2,0,1:T(8,128)}, u32[]{:S(2)}, u32[]{:S(2)}) collective-permute-start(f32[32,1,2048]{2,0,1:T(8,128)S(1)} %bitcast.182), channel_id=1, source_target_pairs={{0,16},{16,32},{32,48},{48,64},{64,80},{80,96},{96,112},{112,128},... | collective-permute-start | bytes 786440 | tf_op jit(solution)/shard_map/while/body/eval_jaxpr/ppermute | solution.py:23
  319.3 11.6 %collective-permute-start.1 = (f32[32,1,2048]{2,0,1:T(8,128)S(1)}, f32[32,1,2048]{2,0,1:T(8,128)}, u32[]{:S(2)}, u32[]{:S(2)}) collective-permute-start(f32[32,1,2048]{2,0,1:T(8,128)S(1)} %bitcast.183), channel_id=1, source_target_pairs={{16,0},{32,16},{48,32},{64,48},{80,64},{96,80},{112,96},{128,112},... | collective-permute-start | bytes 786440 | tf_op jit(solution)/shard_map/while/body/eval_jaxpr/ppermute | solution.py:26
  350.6 16.9 %collective-permute-start = (f32[32,1,2048]{2,0,1:T(8,128)S(1)}, f32[32,1,2048]{2,0,1:T(8,128)}, u32[]{:S(2)}, u32[]{:S(2)}) collective-permute-start(f32[32,1,2048]{2,0,1:T(8,128)S(1)} %bitcast.182), channel_id=1, source_target_pairs={{0,16},{16,32},{32,48},{48,64},{64,80},{80,96},{96,112},{112,128},... | collective-permute-start | bytes 786440 | tf_op jit(solution)/shard_map/while/body/eval_jaxpr/ppermute | solution.py:23
  355.9 11.6 %collective-permute-start.1 = (f32[32,1,2048]{2,0,1:T(8,128)S(1)}, f32[32,1,2048]{2,0,1:T(8,128)}, u32[]{:S(2)}, u32[]{:S(2)}) collective-permute-start(f32[32,1,2048]{2,0,1:T(8,128)S(1)} %bitcast.183), channel_id=1, source_target_pairs={{16,0},{32,16},{48,32},{64,48},{80,64},{96,80},{112,96},{128,112},... | collective-permute-start | bytes 786440 | tf_op jit(solution)/shard_map/while/body/eval_jaxpr/ppermute | solution.py:26
  394.8 16.8 %collective-permute-start.2 = (f32[32,1,2048]{2,0,1:T(8,128)S(1)}, f32[32,1,2048]{2,0,1:T(8,128)}, u32[]{:S(2)}, u32[]{:S(2)}) collective-permute-start(f32[32,1,2048]{2,0,1:T(8,128)S(1)} %bitcast.185), channel_id=1, source_target_pairs={{0,16},{16,32},{32,48},{48,64},{64,80},{80,96},{96,112},{112,128},... | collective-permute-start | bytes 786440 | tf_op jit(solution)/shard_map/while/body/eval_jaxpr/ppermute | solution.py:23
  400.1 11.6 %collective-permute-start.3 = (f32[32,1,2048]{2,0,1:T(8,128)S(1)}, f32[32,1,2048]{2,0,1:T(8,128)}, u32[]{:S(2)}, u32[]{:S(2)}) collective-permute-start(f32[32,1,2048]{2,0,1:T(8,128)S(1)} %bitcast.186), channel_id=1, source_target_pairs={{16,0},{32,16},{48,32},{64,48},{80,64},{96,80},{112,96},{128,112},... | collective-permute-start | bytes 786440 | tf_op jit(solution)/shard_map/while/body/eval_jaxpr/ppermute | solution.py:26
  431.0 17.1 %collective-permute-start.2 = (f32[32,1,2048]{2,0,1:T(8,128)S(1)}, f32[32,1,2048]{2,0,1:T(8,128)}, u32[]{:S(2)}, u32[]{:S(2)}) collective-permute-start(f32[32,1,2048]{2,0,1:T(8,128)S(1)} %bitcast.185), channel_id=1, source_target_pairs={{0,16},{16,32},{32,48},{48,64},{64,80},{80,96},{96,112},{112,128},... | collective-permute-start | bytes 786440 | tf_op jit(solution)/shard_map/while/body/eval_jaxpr/ppermute | solution.py:23
  436.5 11.6 %collective-permute-start.3 = (f32[32,1,2048]{2,0,1:T(8,128)S(1)}, f32[32,1,2048]{2,0,1:T(8,128)}, u32[]{:S(2)}, u32[]{:S(2)}) collective-permute-start(f32[32,1,2048]{2,0,1:T(8,128)S(1)} %bitcast.186), channel_id=1, source_target_pairs={{16,0},{32,16},{48,32},{64,48},{80,64},{96,80},{112,96},{128,112},... | collective-permute-start | bytes 786440 | tf_op jit(solution)/shard_map/while/body/eval_jaxpr/ppermute | solution.py:26
  467.8 17.3 %collective-permute-start.2 = (f32[32,1,2048]{2,0,1:T(8,128)S(1)}, f32[32,1,2048]{2,0,1:T(8,128)}, u32[]{:S(2)}, u32[]{:S(2)}) collective-permute-start(f32[32,1,2048]{2,0,1:T(8,128)S(1)} %bitcast.185), channel_id=1, source_target_pairs={{0,16},{16,32},{32,48},{48,64},{64,80},{80,96},{96,112},{112,128},... | collective-permute-start | bytes 786440 | tf_op jit(solution)/shard_map/while/body/eval_jaxpr/ppermute | solution.py:23
  473.5 11.6 %collective-permute-start.3 = (f32[32,1,2048]{2,0,1:T(8,128)S(1)}, f32[32,1,2048]{2,0,1:T(8,128)}, u32[]{:S(2)}, u32[]{:S(2)}) collective-permute-start(f32[32,1,2048]{2,0,1:T(8,128)S(1)} %bitcast.186), channel_id=1, source_target_pairs={{16,0},{32,16},{48,32},{64,48},{80,64},{96,80},{112,96},{128,112},... | collective-permute-start | bytes 786440 | tf_op jit(solution)/shard_map/while/body/eval_jaxpr/ppermute | solution.py:26
  504.8 17.3 %collective-permute-start.2 = (f32[32,1,2048]{2,0,1:T(8,128)S(1)}, f32[32,1,2048]{2,0,1:T(8,128)}, u32[]{:S(2)}, u32[]{:S(2)}) collective-permute-start(f32[32,1,2048]{2,0,1:T(8,128)S(1)} %bitcast.185), channel_id=1, source_target_pairs={{0,16},{16,32},{32,48},{48,64},{64,80},{80,96},{96,112},{112,128},... | collective-permute-start | bytes 786440 | tf_op jit(solution)/shard_map/while/body/eval_jaxpr/ppermute | solution.py:23
  510.6 11.6 %collective-permute-start.3 = (f32[32,1,2048]{2,0,1:T(8,128)S(1)}, f32[32,1,2048]{2,0,1:T(8,128)}, u32[]{:S(2)}, u32[]{:S(2)}) collective-permute-start(f32[32,1,2048]{2,0,1:T(8,128)S(1)} %bitcast.186), channel_id=1, source_target_pairs={{16,0},{32,16},{48,32},{64,48},{80,64},{96,80},{112,96},{128,112},... | collective-permute-start | bytes 786440 | tf_op jit(solution)/shard_map/while/body/eval_jaxpr/ppermute | solution.py:26
  541.8 17.5 %collective-permute-start.2 = (f32[32,1,2048]{2,0,1:T(8,128)S(1)}, f32[32,1,2048]{2,0,1:T(8,128)}, u32[]{:S(2)}, u32[]{:S(2)}) collective-permute-start(f32[32,1,2048]{2,0,1:T(8,128)S(1)} %bitcast.185), channel_id=1, source_target_pairs={{0,16},{16,32},{32,48},{48,64},{64,80},{80,96},{96,112},{112,128},... | collective-permute-start | bytes 786440 | tf_op jit(solution)/shard_map/while/body/eval_jaxpr/ppermute | solution.py:23
  547.7 11.6 %collective-permute-start.3 = (f32[32,1,2048]{2,0,1:T(8,128)S(1)}, f32[32,1,2048]{2,0,1:T(8,128)}, u32[]{:S(2)}, u32[]{:S(2)}) collective-permute-start(f32[32,1,2048]{2,0,1:T(8,128)S(1)} %bitcast.186), channel_id=1, source_target_pairs={{16,0},{32,16},{48,32},{64,48},{80,64},{96,80},{112,96},{128,112},... | collective-permute-start | bytes 786440 | tf_op jit(solution)/shard_map/while/body/eval_jaxpr/ppermute | solution.py:26
  579.0 19.7 %collective-permute-start.2 = (f32[32,1,2048]{2,0,1:T(8,128)S(1)}, f32[32,1,2048]{2,0,1:T(8,128)}, u32[]{:S(2)}, u32[]{:S(2)}) collective-permute-start(f32[32,1,2048]{2,0,1:T(8,128)S(1)} %bitcast.185), channel_id=1, source_target_pairs={{0,16},{16,32},{32,48},{48,64},{64,80},{80,96},{96,112},{112,128},... | collective-permute-start | bytes 786440 | tf_op jit(solution)/shard_map/while/body/eval_jaxpr/ppermute | solution.py:23
  587.2 11.6 %collective-permute-start.3 = (f32[32,1,2048]{2,0,1:T(8,128)S(1)}, f32[32,1,2048]{2,0,1:T(8,128)}, u32[]{:S(2)}, u32[]{:S(2)}) collective-permute-start(f32[32,1,2048]{2,0,1:T(8,128)S(1)} %bitcast.186), channel_id=1, source_target_pairs={{16,0},{32,16},{48,32},{64,48},{80,64},{96,80},{112,96},{128,112},... | collective-permute-start | bytes 786440 | tf_op jit(solution)/shard_map/while/body/eval_jaxpr/ppermute | solution.py:26
  637.2 17.5 %collective-permute-start.6 = (f32[64,1,2048]{2,0,1:T(8,128)S(1)}, f32[64,1,2048]{2,0,1:T(8,128)S(1)}, u32[]{:S(2)}, u32[]{:S(2)}) collective-permute-start(f32[64,1,2048]{2,0,1:T(8,128)S(1)} %maximum_bitcast_fusion), channel_id=1, source_target_pairs={{0,16},{16,32},{32,48},{48,64},{64,80},{80,96},{96,112},{112,128},... | collective-permute-start | bytes 1572872 | tf_op jit(solution)/shard_map/ppermute | solution.py:23
  644.7 14.7 %collective-permute-start.7 = (f32[64,1,2048]{2,0,1:T(8,128)S(1)}, f32[64,1,2048]{2,0,1:T(8,128)S(1)}, u32[]{:S(2)}, u32[]{:S(2)}) collective-permute-start(f32[64,1,2048]{2,0,1:T(8,128)S(1)} %maximum_bitcast_fusion), channel_id=1, source_target_pairs={{16,0},{32,16},{48,32},{64,48},{80,64},{96,80},{112,96},{128,112},... | collective-permute-start | bytes 1572872 | tf_op jit(solution)/shard_map/ppermute | solution.py:26
  673.0 173.8 %copy-start.32 = (f32[512,32]{0,1:T(8,128)S(1)}, f32[512,32]{0,1:T(8,128)}, u32[]{:S(2)}) copy-start(f32[512,32]{0,1:T(8,128)} %param.15) | copy-start | bytes 196612
  673.0 173.8 %copy-start.47 = (f32[512,32]{0,1:T(8,128)S(1)}, f32[512,32]{0,1:T(8,128)}, u32[]{:S(2)}) copy-start(f32[512,32]{0,1:T(8,128)} %param.25) | copy-start | bytes 196612
  (118 other events, 1075.6 us)
Sparse Core Ops, SparseCore 0:
  11.2 124.0 all-reduce.18
  679.9 166.8 all-reduce.20
where the time goes:
time: 861 us; the launch traced here: 857 us
  other arithmetic  338 us (39%)
  waiting for transfers between devices  294 us (34%)
  local copies, waits for them, and re-layouts  106 us (12%)
  starting transfers between devices  98 us (11%)
  between operations  14.6 us (2%)
    psum x1, waiting for transfers between devices, body(): mode_grad = lax.psum(grad_rows, 'cells')  166 us
    psum x1, waiting for transfers between devices, body(): partial_field = lax.psum(local_field, 'modes')  123 us
    scatter-add x24, other arithmetic, operate(): result = result.at[:, near_cell].add(flux_n).at[:, far_cell].add(-flux_n)  98.5 us
    ppermute x14, starting transfers between devices, extended(): lax.ppermute(lax.slice_in_dim(block, block.shape[dim] - width, None, axis...  79.8 us
    add x12, other arithmetic, sweep_step(): direction = rho_next * rho * direction + 2.0 * rho_next / half * resid  50.3 us
    sub x12, other arithmetic, operate(): result = result + pad_axis(flux_z, 3, 0, 1) - pad_axis(flux_z, 3, 1, 0)  36.9 us
    gather x24, local copies, waits for them, and re-layouts, operate(): flux_n = trans_n * (flat[:, near_cell] - flat[:, far_cell])  35.2 us
    mul x12, other arithmetic, operate(): flux_z = trans_z * (field[..., :-1] - field[..., 1:])  29.7 us
  transfers between devices with their start and end apart: 30, of which 3 were waited for; matrix products, arithmetic and copies ran while one was open for 15% of the time, Pallas kernels for 0%

commit v1 on v0

v1 whole, which is shorter than its diff:
```python
import math

import jax
import jax.numpy as jnp
from jax import lax
from jax.experimental import pallas as pl
from jax.experimental.pallas import tpu as pltpu
from jax.sharding import PartitionSpec as P

NY = 32
NZ = 64
SWEEPS = 6
LAYERS = 16
LANES = 128
ROWS = NY * NZ // LANES
SLOT_ROWS = 2
PIECE = 48
THROWS = 3

LOW_EIG = 0.1
HIGH_EIG = 1.9
STEP_SIZE = 0.01
AXES = ("cells", "modes")
VMEM = pl.BlockSpec(memory_space=pltpu.VMEM)
SMEM = pl.BlockSpec(memory_space=pltpu.SMEM)


def cost(flops, bytes_accessed):
    return pl.CostEstimate(flops=flops, bytes_accessed=bytes_accessed, transcendentals=0)


def chebyshev():
    center = 0.5 * (HIGH_EIG + LOW_EIG)
    half = 0.5 * (HIGH_EIG - LOW_EIG)
    sigma = center / half
    rho = 1.0 / sigma
    factors = []
    for _ in range(SWEEPS):
        rho_next = 1.0 / (2.0 * sigma - rho)
        factors.append((rho_next * rho, 2.0 * rho_next / half))
        rho = rho_next
    return center, factors


CENTER, FACTORS = chebyshev()


def field_kernel(theta_ref, basis_ref, out_ref):
    theta_b = theta_ref[...].astype(jnp.bfloat16)
    part = lax.dot_general(
        theta_b, basis_ref[...], (((1,), (1,)), ((), ())), preferred_element_type=jnp.float32
    )
    for row in range(out_ref.shape[1]):
        out_ref[:, row, :] = part[:, row * LANES : (row + 1) * LANES]


def field_of(theta, basis):
    chains, modes = theta.shape
    steps = 2
    return pl.pallas_call(
        field_kernel,
        grid=(steps,),
        in_specs=[
            pl.BlockSpec((chains, modes), lambda i: (0, 0)),
            pl.BlockSpec((ROWS * LANES // steps, modes), lambda i: (i, 0)),
        ],
        out_specs=pl.BlockSpec((chains, ROWS // steps, LANES), lambda i: (0, i, 0)),
        out_shape=jax.ShapeDtypeStruct((chains, ROWS, LANES), jnp.float32),
        cost_estimate=cost(2 * chains * modes * ROWS * LANES, 2 * modes * ROWS * LANES),
        name="field",
    )(theta, basis)


def left_half():
    return lax.broadcasted_iota(jnp.int32, (ROWS, LANES), 1) < NZ


def swap(a):
    return pltpu.roll(a, NZ, 1)


def span(low, high):
    return low, (high - low) / 65535.0


MULT_SPAN, STORE_SPAN, WELL_SPAN, UNIT_SPAN = (
    span(0.3, 3.0),
    span(0.05, 0.5),
    span(-6.0, 6.0),
    span(0.1, 1.0),
)


def code16(a, within):
    low, step = within
    return ((a - low) * (1.0 / step) + 0.5).astype(jnp.int32) - 32768


def value16(code, within):
    low, step = within
    return (code + 32768).astype(jnp.float32) * step + low


def pack(high, low):
    return (high << 16) | (low & 0xFFFF)


def high16(word):
    return word >> 16


def low16(word):
    return (word << 16) >> 16


def combine_kernel(
    place_ref,
    parts_ref,
    mean_ref,
    face_ref,
    storage_ref,
    sources_ref,
    data_ref,
    weight_ref,
    pairs_ref,
    fault_ref,
    out_ref,
):
    total = jnp.sum(parts_ref[...], axis=0)
    mean = mean_ref[...]
    first, second = total[0] + mean, total[1] + mean
    left = left_half()
    even = jnp.where(left, first, swap(second))
    odd = jnp.where(left, swap(first), second)
    top = jnp.max(jnp.maximum(jnp.abs(even), jnp.abs(odd)), axis=(0, 1), keepdims=True)
    bound = (top * 256.0).astype(jnp.int32) + 1
    factor = (32767.0 * 256.0) / bound.astype(jnp.float32)

    def scaled(a):
        return jnp.floor(a * factor + 0.5).astype(jnp.int32)

    def rows_of(a):
        return jnp.concatenate(
            [a[:, row * LANES : (row + 1) * LANES] for row in range(a.shape[1] // LANES)], 0
        )

    face = face_ref[...]
    mult = [code16(rows_of(face[k : k + 1]), MULT_SPAN) for k in range(3)]
    store = code16(storage_ref[...], STORE_SPAN)
    source = code16(sources_ref[...], WELL_SPAN)
    data = code16(data_ref[...], WELL_SPAN)
    weight = code16(weight_ref[...], UNIT_SPAN)
    near, far = rows_of(pairs_ref[0:1]), rows_of(pairs_ref[1:2])
    code = near * 4 + jnp.where(near == far, 0, far - near - NZ)
    fault = code16(rows_of(fault_ref[...]), UNIT_SPAN)
    bounds = jnp.broadcast_to(bound, (2, LANES))
    zeros = jnp.zeros((2, LANES), jnp.int32)
    forms = (
        [
            pack(mult[0], mult[1]),
            pack(mult[2][0:8], mult[2][8:16]),
            pack(store[0:4], store[4:8]),
            zeros,
            bounds,
        ],
        [
            pack(source, data),
            pack(weight[0:8], weight[8:16]),
            pack(store[8:12], store[12:16]),
            pack(code, fault),
            bounds,
        ],
    )
    forms = [jnp.concatenate(form, 0) for form in forms]
    fixed = jnp.where(place_ref[1] == 0, forms[0], forms[1])
    field = pack(scaled(even), scaled(odd))
    for k in range(out_ref.shape[0]):
        out_ref[k, 0:ROWS] = field
        out_ref[k, ROWS:PIECE] = fixed


def combine(place, parts, *fixed):
    return pl.pallas_call(
        combine_kernel,
        in_specs=[SMEM] + [VMEM] * (1 + len(fixed)),
        out_specs=VMEM,
        out_shape=jax.ShapeDtypeStruct((LAYERS, PIECE, LANES), jnp.int32),
        cost_estimate=cost(2**17, 2**20),
        name="combine",
    )(place, parts, *fixed)


def harmonic(left, right):
    return 2.0 * left * right / (left + right)


def ahead(a, s):
    return pltpu.roll(a, LANES - s, 1)


def behind(a, s):
    return pltpu.roll(a, s, 1)


def up(a):
    return pltpu.roll(a, ROWS - 1, 0)


def down(a):
    return pltpu.roll(a, 1, 0)


def spread(a):
    left, other = left_half(), swap(a)
    return jnp.where(left, a, other), jnp.where(left, other, a)


def neighbours(even, odd, above, below):
    to_even = [above[0], below[0], ahead(even, 1), behind(even, 1), odd, down(odd)]
    to_odd = [above[1], below[1], ahead(odd, 1), behind(odd, 1), up(even), even]
    for s in range(1, THROWS + 1):
        to_even.append(ahead(odd, s))
        to_odd.append(up(ahead(even, s)))
    for s in range(1, THROWS + 1):
        to_even.append(down(behind(odd, s)))
        to_odd.append(behind(even, s))
    return to_even, to_odd


def physics_kernel(
    place_ref,
    own_ref,
    other_ref,
    pressure_ref,
    glogk_ref,
    perm,
    coef,
    inverse,
    local,
    weight,
    data,
    resid,
    field,
    adjoint,
    dir_a,
    dir_b,
):
    here, core = place_ref[0], place_ref[1]
    zeros = jnp.zeros((ROWS, LANES), jnp.float32)
    for pad in (0, LAYERS + 1):
        for k in range(2):
            perm[pad, k] = zeros + 1.0
            field[pad, k] = zeros
            adjoint[pad, k] = zeros
            dir_a[pad, k] = zeros
            dir_b[pad, k] = zeros
    for x in range(LAYERS):
        word = own_ref[x, 0:ROWS]
        factor = own_ref[x, PIECE - 1 : PIECE].astype(jnp.float32) * (1.0 / (32767.0 * 256.0))
        perm[x + 1, 0] = jnp.exp(high16(word).astype(jnp.float32) * factor)
        perm[x + 1, 1] = jnp.exp(low16(word).astype(jnp.float32) * factor)

    lane = lax.broadcasted_iota(jnp.int32, (ROWS, LANES), 1)
    row = lax.broadcasted_iota(jnp.int32, (ROWS, LANES), 0)
    z_inside = (lane & (NZ - 1)) < NZ - 1
    y_inside = row < ROWS - 1
    keys = lax.broadcasted_iota(jnp.int32, (THROWS * ROWS, LANES), 0)
    lanes_of = lax.broadcasted_iota(jnp.int32, (LANES, LANES), 0)

    def prepare(x, carry):
        own, other = own_ref[x, ROWS:PIECE], other_ref[x, ROWS:PIECE]
        first = jnp.where(core == 0, own, other)
        second = jnp.where(core == 0, other, own)
        mult_x = spread(value16(high16(first[0:16]), MULT_SPAN))
        mult_y = spread(value16(low16(first[0:16]), MULT_SPAN))
        halves = (high16(first[16:24]), low16(first[16:24]))
        mult_z = spread(value16(jnp.concatenate(halves, 0), MULT_SPAN))
        store = [op(w[24:28]) for w in (first, second) for op in (high16, low16)]
        storage = spread(value16(jnp.concatenate(store, 0), STORE_SPAN))
        source = spread(value16(high16(second[0:16]), WELL_SPAN))
        obs_data = spread(value16(low16(second[0:16]), WELL_SPAN))
        halves = (high16(second[16:24]), low16(second[16:24]))
        obs_weight = spread(value16(jnp.concatenate(halves, 0), UNIT_SPAN))
        slots = second[28:30]
        faults = jnp.zeros((THROWS * ROWS, LANES), jnp.float32)
        for h in range(SLOT_ROWS):
            code = high16(slots[h : h + 1])
            throw, cell = code & 3, code >> 2
            key = jnp.where(throw > 0, (throw - 1) * ROWS + (cell >> 7), -1)
            amount = value16(low16(slots[h : h + 1]), UNIT_SPAN)
            rows_hot = jnp.where(keys == key, amount, 0.0)
            lanes_hot = jnp.where(lanes_of == (cell & (LANES - 1)), 1.0, 0.0).astype(jnp.bfloat16)
            for _ in range(3):
                piece = rows_hot.astype(jnp.bfloat16)
                faults = faults + lax.dot_general(
                    piece, lanes_hot, (((1,), (1,)), ((), ())), preferred_element_type=jnp.float32
                )
                rows_hot = rows_hot - piece.astype(jnp.float32)
        even, odd = perm[x + 1, 0], perm[x + 1, 1]
        inside = jnp.where(x < LAYERS - 1, 1.0, 0.0)
        xp_even = harmonic(even, perm[x + 2, 0]) * mult_x[0] * inside
        xp_odd = harmonic(odd, perm[x + 2, 1]) * mult_x[1] * inside
        xm_even, xm_odd = carry
        zp_even = jnp.where(z_inside, harmonic(even, ahead(even, 1)) * mult_z[0], 0.0)
        zp_odd = jnp.where(z_inside, harmonic(odd, ahead(odd, 1)) * mult_z[1], 0.0)
        y_even = harmonic(even, odd) * mult_y[0]
        y_odd = jnp.where(y_inside, harmonic(odd, up(even)) * mult_y[1], 0.0)
        to_even = [xp_even, xm_even, zp_even, behind(zp_even, 1), y_even, down(y_odd)]
        to_odd = [xp_odd, xm_odd, zp_odd, behind(zp_odd, 1), y_odd, y_even]
        back_even, back_odd = [], []
        for s in range(1, THROWS + 1):
            fault = spread(faults[(s - 1) * ROWS : s * ROWS])
            fault_even = harmonic(even, ahead(odd, s)) * fault[0]
            fault_odd = harmonic(odd, up(ahead(even, s))) * fault[1]
            to_even.append(fault_even)
            to_odd.append(fault_odd)
            back_even.append(down(behind(fault_odd, s)))
            back_odd.append(behind(fault_even, s))
        to_even += back_even
        to_odd += back_odd

        @pl.when(x == here)
        def _():
            for k in range(12):
                local[k, 0] = to_even[k]
                local[k, 1] = to_odd[k]

        for side, trans in ((0, to_even), (1, to_odd)):
            diag = storage[side]
            for t in trans:
                diag = diag + t
            inv = 1.0 / diag
            inverse[x, side] = inv
            for k in range(12):
                value = trans[k] * inv
                if side == 0 and k in (5, 9, 10, 11):
                    value = up(value)
                if side == 1 and k in (4, 6, 7, 8):
                    value = down(value)
                coef[x, k, side] = value
            weight[x, side] = obs_weight[side]
            data[x, side] = obs_data[side]
            start = source[side] * inv
            resid[x, side] = start
            dir_a[x + 1, side] = start * (1.0 / CENTER)
            field[x + 1, side] = zeros
        return xp_even, xp_odd

    lax.fori_loop(0, LAYERS, prepare, (zeros, zeros))

    def sweep(total, source_dir, target_dir, keep, gain):
        for x in range(LAYERS):
            even, odd = source_dir[x + 1, 0], source_dir[x + 1, 1]
            c = lambda k, side: coef[x, k, side]
            acc_even = c(0, 0) * source_dir[x + 2, 0] + c(1, 0) * source_dir[x, 0]
            acc_odd = c(0, 1) * source_dir[x + 2, 1] + c(1, 1) * source_dir[x, 1]
            acc_even += c(4, 0) * odd
            acc_odd += c(5, 1) * even
            low = c(5, 0) * odd
            high = c(4, 1) * even
            for s in range(1, THROWS + 1):
                even_ahead, odd_ahead = ahead(even, s), ahead(odd, s)
                even_behind, odd_behind = behind(even, s), behind(odd, s)
                if s == 1:
                    acc_even += c(2, 0) * even_ahead + c(3, 0) * even_behind
                    acc_odd += c(2, 1) * odd_ahead + c(3, 1) * odd_behind
                acc_even += c(5 + s, 0) * odd_ahead
                acc_odd += c(8 + s, 1) * even_behind
                low += c(8 + s, 0) * odd_behind
                high += c(5 + s, 1) * even_ahead
            acc_even += down(low)
            acc_odd += up(high)
            for side, own, acc in ((0, even, acc_even), (1, odd, acc_odd)):
                left = resid[x, side] - (own - acc)
                resid[x, side] = left
                total[x + 1, side] = total[x + 1, side] + own
                target_dir[x + 1, side] = keep * own + gain * left

    def solve(total):
        def pair(i, carry):
            def pick(k, j):
                return jnp.where(
                    i == 0,
                    FACTORS[k][j],
                    jnp.where(i == 1, FACTORS[k + 2][j], FACTORS[k + 4][j]),
                ).astype(jnp.float32)

            sweep(total, dir_a, dir_b, pick(0, 0), pick(0, 1))
            sweep(total, dir_b, dir_a, pick(1, 0), pick(1, 1))
            return carry

        lax.fori_loop(0, SWEEPS // 2, pair, 0)

    solve(field)
    for x in range(LAYERS):
        for side in range(2):
            value = field[x + 1, side] + dir_a[x + 1, side]
            field[x + 1, side] = value
            start = weight[x, side] * (value - data[x, side]) * inverse[x, side]
            resid[x, side] = start
            dir_a[x + 1, side] = start * (1.0 / CENTER)
            adjoint[x + 1, side] = zeros
    solve(adjoint)

    def around(ref, extra=None):
        def read(layer):
            pair = [ref[here + layer, 0], ref[here + layer, 1]]
            if extra is not None:
                pair = [pair[k] + extra[here + layer, k] for k in range(2)]
            return pair

        below, mine, above = read(0), read(1), read(2)
        return mine, neighbours(mine[0], mine[1], above, below)

    perm_mine, perm_next = around(perm)
    pres_mine, pres_next = around(field)
    adj_mine, adj_next = around(adjoint, dir_a)
    glogk = []
    for side in range(2):
        total = zeros
        for k in range(12):
            other = perm_next[side][k]
            rate = (
                -(adj_mine[side] - adj_next[side][k])
                * (pres_mine[side] - pres_next[side][k])
                * local[k, side]
                / (perm_mine[side] + other)
            )
            total = total + rate * other
        glogk.append(total)

    def apart(even, odd):
        left = left_half()
        return jnp.where(left, even, swap(odd)), jnp.where(left, swap(even), odd)

    first, second = apart(*pres_mine)
    pressure_ref[0] = first
    pressure_ref[1] = second
    first, second = apart(*glogk)
    first, second = first.astype(jnp.bfloat16), second.astype(jnp.bfloat16)
    for m in range(glogk_ref.shape[0]):
        glogk_ref[m, 0] = first
        glogk_ref[m, 1] = second


def physics(place, own, other, copies):
    f32 = jnp.float32

    def buffer(*lead):
        return pltpu.VMEM((*lead, ROWS, LANES), f32)

    padded = LAYERS + 2
    return pl.pallas_call(
        physics_kernel,
        in_specs=[SMEM] + [VMEM] * 2,
        out_specs=[VMEM, VMEM],
        out_shape=[
            jax.ShapeDtypeStruct((2, ROWS, LANES), f32),
            jax.ShapeDtypeStruct((copies, 2, ROWS, LANES), jnp.bfloat16),
        ],
        scratch_shapes=[
            buffer(padded, 2),
            buffer(LAYERS, 12, 2),
            buffer(LAYERS, 2),
            buffer(12, 2),
            buffer(LAYERS, 2),
            buffer(LAYERS, 2),
            buffer(LAYERS, 2),
            buffer(padded, 2),
            buffer(padded, 2),
            buffer(padded, 2),
            buffer(padded, 2),
        ],
        compiler_params=pltpu.CompilerParams(vmem_limit_bytes=24 * 2**20),
        cost_estimate=cost(2**32, 2**24),
        name="physics",
    )(place, own, other)


def gradient_kernel(glogk_ref, basis_ref, out_ref, rows):
    chains = out_ref.shape[0]
    values = glogk_ref[...].astype(jnp.float32).reshape(chains, ROWS, LANES)
    rows[...] = values
    for row in range(ROWS):
        left = rows[:, row, :].astype(jnp.bfloat16)
        part = jnp.dot(
            left,
            basis_ref[row * LANES : (row + 1) * LANES, :],
            preferred_element_type=jnp.float32,
        )
        if row == 0:
            out_ref[...] = part
        else:
            out_ref[...] += part


def gradient_of(glogk, basis):
    chains = glogk.shape[0] * glogk.shape[1]
    return pl.pallas_call(
        gradient_kernel,
        in_specs=[VMEM, VMEM],
        out_specs=VMEM,
        out_shape=jax.ShapeDtypeStruct((chains, basis.shape[1]), jnp.float32),
        scratch_shapes=[pltpu.VMEM((chains, ROWS, LANES), jnp.float32)],
        compiler_params=pltpu.CompilerParams(vmem_limit_bytes=16 * 2**20),
        cost_estimate=cost(2 * chains * basis.size, 2 * basis.size),
        name="gradient",
    )(glogk, basis)


def copies_kernel(one_ref, two_ref, out_ref):
    total = (one_ref[...] + two_ref[...]).astype(jnp.bfloat16)
    for k in range(out_ref.shape[0]):
        out_ref[k] = total


def copies_of(one, two, count):
    return pl.pallas_call(
        copies_kernel,
        in_specs=[VMEM, VMEM],
        out_specs=VMEM,
        out_shape=jax.ShapeDtypeStruct((count, *one.shape), jnp.bfloat16),
        cost_estimate=cost(2**16, 2**19),
        name="copies",
    )(one, two)


def exchange(value, mask, size):
    return lax.ppermute(value, AXES, [(i, i ^ mask) for i in range(size)])


def body(
    theta,
    basis,
    mean_logk,
    face_mult,
    storage,
    sources,
    obs_data,
    obs_weight,
    fault_pairs,
    fault_mult,
    noise,
):
    modes_n, cells_n = lax.axis_size("modes"), lax.axis_size("cells")
    size = cells_n * modes_n
    here = lax.axis_index("cells")
    core = lax.axis_index("modes") & 1
    place = jnp.stack([here, core]).astype(jnp.int32)

    partial_field = field_of(theta.T, basis).reshape(modes_n, 2, ROWS, LANES)
    parts = lax.all_to_all(partial_field, "modes", 0, 0)
    pieces = combine(
        place,
        parts,
        mean_logk.reshape(ROWS, LANES),
        face_mult,
        storage.reshape(ROWS, LANES),
        sources.reshape(ROWS, LANES),
        obs_data.reshape(ROWS, LANES),
        obs_weight.reshape(ROWS, LANES),
        fault_pairs.T,
        fault_mult.reshape(1, SLOT_ROWS * LANES),
    )
    pieces = lax.all_to_all(pieces, "cells", 0, 0)
    others = exchange(pieces, 1, size)
    pressure, glogk = physics(place, pieces, others, modes_n)
    glogk = lax.all_to_all(glogk, "modes", 0, 0)
    grad_rows = gradient_of(glogk, basis)
    half = cells_n // 2
    grad_rows = copies_of(grad_rows, exchange(grad_rows, half * modes_n, size), half)
    groups = [list(range(half)), list(range(half, cells_n))]
    grad_rows = lax.all_to_all(grad_rows, "cells", 0, 0, axis_index_groups=groups)
    grad = jnp.sum(grad_rows.astype(jnp.float32), 0).T
    theta_next = theta - STEP_SIZE * (grad + theta) + math.sqrt(2.0 * STEP_SIZE) * noise
    return (theta_next, grad, pressure.reshape(2, NY * NZ))


def solution(mesh):
    return jax.shard_map(
        body,
        mesh=mesh,
        in_specs=(
            P("modes", None),
            P("cells", "modes"),
            P("cells"),
            P(None, "cells"),
            P("cells"),
            P("cells"),
            P("cells"),
            P("cells"),
            P("cells", None),
            P("cells"),
            P("modes", None),
        ),
        out_specs=(P("modes", None), P("modes", None), P("modes", "cells")),
        check_vma=False,
    )
```

time: 861 us -> 94.1 us (0.11)
  other arithmetic: 338 us -> 1.27 us
  waiting for transfers between devices: 294 us -> 23.2 us
  local copies, waits for them, and re-layouts: 106 us -> 2.62 us
  starting transfers between devices: 98 us -> 10.4 us
  blocking collectives: 0 us -> 34.6 us
  Pallas kernels: 0 us -> 20.4 us
  between operations: 14.6 us -> 0.69 us
    psum x2 -> x0, waiting for transfers between devices: 289 us -> none  [the longest x1 166 us: body(): mode_grad = lax.psum(grad_rows, 'cells')]
    scatter-add x28 -> x0, other arithmetic: 112 us -> none  [the longest x24 98.5 us: operate(): result = result.at[:, near_cell].add(flux_n).at[:, far_cell].add(-flux_n)]
    ppermute x28 -> x2, starting transfers between devices: 97.9 us -> 0.63 us  [exchange(): return lax.ppermute(value, AXES, [(i, i ^ mask) for i in range(size)])]
    mul x45 -> x0, other arithmetic: 70.6 us -> none  [the longest x12 29.7 us: operate(): flux_z = trans_z * (field[..., :-1] - field[..., 1:])]
    add x17 -> x0, other arithmetic: 59.4 us -> none  [the longest x12 50.3 us: sweep_step(): direction = rho_next * rho * direction + 2.0 * rho_next / half * resid]
    gather x30 -> x0, local copies, waits for them, and re-layouts: 48.2 us -> none  [the longest x24 35.2 us: operate(): flux_n = trans_n * (flat[:, near_cell] - flat[:, far_cell])]
    sub x24 -> x0, other arithmetic: 37.3 us -> none  [the longest x12 36.9 us: operate(): result = result + pad_axis(flux_z, 3, 0, 1) - pad_axis(flux_z, 3, 1, 0)]
    all_to_all x0 -> x2, blocking collectives: none -> 34.6 us  [the longest x1 24.8 us: body(): pieces = lax.all_to_all(pieces, 'cells', 0, 0)]
  transfers between devices with their start and end apart: 30 -> 4, of which waited for: 3 -> 4; matrix products, arithmetic and copies ran while one was open for 15% -> 1% of each run, Pallas kernels for 0% -> 0%
where the time goes in v1:
time: 94.1 us; the launch traced here: 93.3 us
  blocking collectives  34.6 us (37%)
  waiting for transfers between devices  23.2 us (25%)
  Pallas kernels  20.4 us (22%)
  starting transfers between devices  10.4 us (11%)
  local copies, waits for them, and re-layouts  2.62 us (3%)
  other arithmetic  1.27 us (1%)
    all_to_all x1, blocking collectives, body(): pieces = lax.all_to_all(pieces, 'cells', 0, 0)  24.8 us
    pallas_call x1, Pallas kernels, physics(): pl.pallas_call(physics_kernel, in_specs=[SMEM] + [VMEM] * 2, out_specs=[V...  13.6 us
    all_to_all x1, waiting for transfers between devices, body(): lax.all_to_all(grad_rows, 'cells', 0, 0, axis_index_groups=groups)  10.5 us
    all_to_all x1, blocking collectives, body(): glogk = lax.all_to_all(glogk, 'modes', 0, 0)  9.78 us
    ppermute x2, waiting for transfers between devices, exchange(): return lax.ppermute(value, AXES, [(i, i ^ mask) for i in range(size)])  6.86 us
    all_to_all x1, waiting for transfers between devices, body(): parts = lax.all_to_all(partial_field, 'modes', 0, 0)  5.92 us
    all_to_all x1, starting transfers between devices, body(): parts = lax.all_to_all(partial_field, 'modes', 0, 0)  5.78 us
    all_to_all x1, starting transfers between devices, body(): lax.all_to_all(grad_rows, 'cells', 0, 0, axis_index_groups=groups)  4.04 us
  transfers between devices with their start and end apart: 4, of which 4 were waited for; matrix products, arithmetic and copies ran while one was open for 1% of the time, Pallas kernels for 0%

profile of v1, /device:TPU:8, one launch (start us, length us, event | category | flops | bytes accessed | tf_op | source)
XLA Modules:
  0.0 93.3 jit_solution(494493848340984250)
XLA Ops:
  0.6 2.8 %field.1 = f32[32,16,128]{2,1,0:T(8,128)} custom-call(f32[32,512]{1,0:T(8,128)} %bitcast.19, bf16[2048,512]{1,0:T(8,128)(2,1)} %basis_ref.3), custom_call_target="tpu_custom_call" | custom-call | flops 67108864 | bytes 2097152 | tf_op jit(solution)/shard_map/field/pallas_call | solution.py:60
  3.5 5.8 %all-to-all-start = ((f32[16,2,16,128]{3,2,1,0:T(8,128)}), f32[16,2,16,128]{3,2,1,0:T(8,128)S(1)}, u32[]{:S(2)}, u32[]{:S(2)}) async-start(f32[16,2,16,128]{3,2,1,0:T(8,128)} %bitcast.18), calls=%async_computation | async-start | bytes 524288 | tf_op jit(solution)/shard_map/all_to_all | solution.py:552
  9.2 0.6 pad_add_fusion.place_ref
  9.8 5.9 %all-to-all-done.parts_ref = f32[16,2,16,128]{3,2,1,0:T(8,128)S(1)} async-done(((f32[16,2,16,128]{3,2,1,0:T(8,128)}), f32[16,2,16,128]{3,2,1,0:T(8,128)S(1)}, u32[]{:S(2)}, u32[]{:S(2)}) %all-to-all-start) | async-done | bytes 262176 | tf_op jit(solution)/shard_map/all_to_all | solution.py:552
  15.7 0.0 copy-start.3
  15.7 0.7 copy-done.3
  16.4 2.0 %combine.1 = s32[16,48,128]{2,1,0:T(8,128)} custom-call(s32[2]{0:T(128)} %pad_add_fusion.place_ref, f32[16,2,16,128]{3,2,1,0:T(8,128)} %copy-done.3, f32[16,128]{1,0:T(8,128)} %bitcast.22, f32[3,2048]{1,0:T(4,128)} %face_ref.1, f32[16,128]{1,0:T(8,128)} %bitcast.23, f32[16,128]{1,0:T(8,128)} %bitcast.24, f32[16,128]{1,0:T(8,128)} %bitcast.25, ...), custom_call_target="tpu_custom_call" | custom-call | flops 131072 | bytes 1048576 | tf_op jit(solution)/shard_map/combine/pallas_call | solution.py:183
  18.4 24.8 %all_to_all.20.own_ref = s32[16,48,128]{2,1,0:T(8,128)S(1)} all-to-all(s32[16,48,128]{2,1,0:T(8,128)} %combine.1), channel_id=1, replica_groups=mesh['cells'=16,'modes'=16] {'cells'}, dimensions={0} | all-to-all | bytes 786432 | tf_op jit(solution)/shard_map/all_to_all | solution.py:565
  43.2 0.0 copy-start
  43.2 0.0 collective-permute-start
  43.2 1.7 %collective-permute-done.other_ref = s32[16,48,128]{2,1,0:T(8,128)S(1)} collective-permute-done((s32[16,48,128]{2,1,0:T(8,128)S(1)}, s32[16,48,128]{2,1,0:T(8,128)S(1)}, u32[]{:S(2)}, u32[]{:S(2)}) %collective-permute-start) | collective-permute-done | bytes 393248 | tf_op jit(solution)/shard_map/ppermute | solution.py:529
  45.0 0.0 copy-start.2
  45.0 0.7 copy-done.2
  45.6 13.6 %physics.1 = (f32[2,16,128]{2,1,0:T(8,128)S(1)}, bf16[16,2,16,128]{3,2,1,0:T(8,128)(2,1)S(1)}) custom-call(s32[2]{0:T(128)S(1)} %copy-done.2, s32[16,48,128]{2,1,0:T(8,128)S(1)} %all_to_all.20.own_ref, s32[16,48,128]{2,1,0:T(8,128)S(1)} %collective-permute-done.other_ref), custom_call_target="tpu_custom_call" | custom-call | flops 4294967296 | bytes 16777216 | tf_op jit(solution)/shard_map/physics/pallas_call | solution.py:453
  59.2 0.0 copy-start.4
  59.2 0.0 copy-start.6
  59.2 9.8 %all_to_all.21.glogk_ref = bf16[16,2,16,128]{3,2,1,0:T(8,128)(2,1)S(1)} all-to-all(bf16[16,2,16,128]{3,2,1,0:T(8,128)(2,1)S(1)} %get-tuple-element.5), channel_id=1, replica_groups=mesh['cells'=16,'modes'=16] {'modes'}, dimensions={0} | all-to-all | bytes 262144 | tf_op jit(solution)/shard_map/all_to_all | solution.py:568
  69.0 0.0 copy-done
  69.0 0.4 gradient.1.one_ref
  69.4 0.6 collective-permute-start.1
  70.1 5.1 %collective-permute-done.1.two_ref = f32[32,512]{1,0:T(8,128)S(1)} collective-permute-done((f32[32,512]{1,0:T(8,128)S(1)}, f32[32,512]{1,0:T(8,128)S(1)}, u32[]{:S(2)}, u32[]{:S(2)}) %collective-permute-start.1) | collective-permute-done | bytes 65568 | tf_op jit(solution)/shard_map/ppermute | solution.py:529
  75.2 0.0 copy-done.1
  75.2 0.6 copy-done.7
  75.8 1.6 %copies.1 = bf16[8,32,512]{2,1,0:T(8,128)(2,1)} custom-call(f32[32,512]{1,0:T(8,128)} %copy-done.1, f32[32,512]{1,0:T(8,128)} %copy-done.7), custom_call_target="tpu_custom_call" | custom-call | flops 65536 | bytes 524288 | tf_op jit(solution)/shard_map/copies/pallas_call | solution.py:518
  77.4 4.0 %all-to-all-start.3 = ((bf16[8,32,512]{2,1,0:T(8,128)(2,1)}), bf16[8,32,512]{2,1,0:T(8,128)(2,1)S(1)}, u32[]{:S(2)}, u32[]{:S(2)}) async-start(bf16[8,32,512]{2,1,0:T(8,128)(2,1)} %copies.1), calls=%async_computation.3 | async-start | bytes 524288 | tf_op jit(solution)/shard_map/all_to_all | solution.py:573
  81.5 0.6 copy.16
  82.1 10.5 %all-to-all-done.3 = bf16[8,32,512]{2,1,0:T(8,128)(2,1)S(1)} async-done(((bf16[8,32,512]{2,1,0:T(8,128)(2,1)}), bf16[8,32,512]{2,1,0:T(8,128)(2,1)S(1)}, u32[]{:S(2)}, u32[]{:S(2)}) %all-to-all-start.3) | async-done | bytes 262176 | tf_op jit(solution)/shard_map/all_to_all | solution.py:573
  92.6 0.0 copy-done.4
  92.6 0.0 copy-done.6
  92.6 0.0 copy-start.5
  92.6 0.7 multiply_add_fusion
  93.3 0.0 copy-done.5
  (3 shorter events, 0.0 us)
Async XLA Ops:
  3.5 12.3 %all-to-all-start = ((f32[16,2,16,128]{3,2,1,0:T(8,128)}), f32[16,2,16,128]{3,2,1,0:T(8,128)S(1)}, u32[]{:S(2)}, u32[]{:S(2)}) async-start(f32[16,2,16,128]{3,2,1,0:T(8,128)} %bitcast.18), calls=%async_computation | async-start | bytes 524288 | tf_op jit(solution)/shard_map/all_to_all | solution.py:552
  15.7 0.7 copy-start.3
  43.2 25.8 %copy-start = (bf16[2048,512]{1,0:T(8,128)(2,1)S(1)}, bf16[2048,512]{1,0:T(8,128)(2,1)}, u32[]{:S(2)}) copy-start(bf16[2048,512]{1,0:T(8,128)(2,1)} %basis_ref.3) | copy-start | bytes 6291460
  43.2 1.7 %collective-permute-start = (s32[16,48,128]{2,1,0:T(8,128)S(1)}, s32[16,48,128]{2,1,0:T(8,128)S(1)}, u32[]{:S(2)}, u32[]{:S(2)}) collective-permute-start(s32[16,48,128]{2,1,0:T(8,128)S(1)} %all_to_all.20.own_ref), channel_id=1, source_target_pairs={{0,1},{1,0},{2,3},{3,2},{4,5},{5,4},{6,7},{7,6},{8,9},{9,8},{10,11... | collective-permute-start | bytes 1179656 | tf_op jit(solution)/shard_map/ppermute | solution.py:529
  45.0 0.7 copy-start.2
  59.2 33.4 %copy-start.4 = (f32[512,32]{0,1:T(8,128)S(1)}, f32[512,32]{0,1:T(8,128)}, u32[]{:S(2)}) copy-start(f32[512,32]{0,1:T(8,128)} %param.11) | copy-start | bytes 196612
  59.2 33.4 %copy-start.6 = (f32[512,32]{0,1:T(8,128)S(1)}, f32[512,32]{0,1:T(8,128)}, u32[]{:S(2)}) copy-start(f32[512,32]{0,1:T(8,128)} %param.21) | copy-start | bytes 196612
  69.4 5.8 %copy-start.1 = (f32[32,512]{1,0:T(8,128)}, f32[32,512]{1,0:T(8,128)S(1)}, u32[]{:S(2)}) copy-start(f32[32,512]{1,0:T(8,128)S(1)} %gradient.1.one_ref) | copy-start | bytes 196612
  69.4 5.8 %collective-permute-start.1 = (f32[32,512]{1,0:T(8,128)S(1)}, f32[32,512]{1,0:T(8,128)S(1)}, u32[]{:S(2)}, u32[]{:S(2)}) collective-permute-start(f32[32,512]{1,0:T(8,128)S(1)} %gradient.1.one_ref), channel_id=1, source_target_pairs={{0,128},{1,129},{2,130},{3,131},{4,132},{5,133},{6,134},{7,135},{8... | collective-permute-start | bytes 196616 | tf_op jit(solution)/shard_map/ppermute | solution.py:529
  75.2 0.6 copy-start.7
  77.4 15.1 %all-to-all-start.3 = ((bf16[8,32,512]{2,1,0:T(8,128)(2,1)}), bf16[8,32,512]{2,1,0:T(8,128)(2,1)S(1)}, u32[]{:S(2)}, u32[]{:S(2)}) async-start(bf16[8,32,512]{2,1,0:T(8,128)(2,1)} %copies.1), calls=%async_computation.3 | async-start | bytes 524288 | tf_op jit(solution)/shard_map/all_to_all | solution.py:573
  92.6 0.7 copy-start.5

commit v2 on v1

--- a/solution.py
+++ b/solution.py
@@ -22,7 +22,10 @@
 STEP_SIZE = 0.01
 AXES = ("cells", "modes")
 VMEM = pl.BlockSpec(memory_space=pltpu.VMEM)
-SMEM = pl.BlockSpec(memory_space=pltpu.SMEM)
+
+
+def place():
+    return lax.axis_index("cells"), lax.axis_index("modes") & 1
 
 
 def cost(flops, bytes_accessed):
@@ -45,30 +48,49 @@
 CENTER, FACTORS = chebyshev()
 
 
-def field_kernel(theta_ref, basis_ref, out_ref):
-    theta_b = theta_ref[...].astype(jnp.bfloat16)
-    part = lax.dot_general(
-        theta_b, basis_ref[...], (((1,), (1,)), ((), ())), preferred_element_type=jnp.float32
-    )
-    for row in range(out_ref.shape[1]):
-        out_ref[:, row, :] = part[:, row * LANES : (row + 1) * LANES]
+def field_kernel(theta_hbm, basis_hbm, out_ref, theta, basis, sems):
+    steps = sems.shape[0] - 1
+    count = basis.shape[0] // steps
+    copies = [pltpu.make_async_copy(theta_hbm, theta, sems.at[steps])]
+    for step in range(steps):
+        rows = pl.ds(step * count, count)
+        copies.append(pltpu.make_async_copy(basis_hbm.at[rows], basis.at[rows], sems.at[step]))
+    for copy in copies:
+        copy.start()
+    copies[0].wait()
+    theta_b = theta[...].astype(jnp.bfloat16)
+    for step in range(steps):
+        copies[step + 1].wait()
+        part = lax.dot_general(
+            theta_b,
+            basis[step * count : (step + 1) * count, :],
+            (((1,), (1,)), ((), ())),
+            preferred_element_type=jnp.float32,
+        )
+        for row in range(count // LANES):
+            out_ref[:, step * (count // LANES) + row, :] = part[:, row * LANES : (row + 1) * LANES]
 
 
 def field_of(theta, basis):
     chains, modes = theta.shape
-    steps = 2
+    steps = 4
     return pl.pallas_call(
         field_kernel,
-        grid=(steps,),
-        in_specs=[
-            pl.BlockSpec((chains, modes), lambda i: (0, 0)),
-            pl.BlockSpec((ROWS * LANES // steps, modes), lambda i: (i, 0)),
+        in_specs=[pl.BlockSpec(memory_space=pltpu.HBM)] * 2,
+        out_specs=VMEM,
+        out_shape=jax.ShapeDtypeStruct((chains, ROWS, LANES), jnp.float32),
+        scratch_shapes=[
+            pltpu.VMEM(theta.shape, theta.dtype),
+            pltpu.VMEM(basis.shape, basis.dtype),
+            pltpu.SemaphoreType.DMA((steps + 1,)),
         ],
-        out_specs=pl.BlockSpec((chains, ROWS // steps, LANES), lambda i: (0, i, 0)),
-        out_shape=jax.ShapeDtypeStruct((chains, ROWS, LANES), jnp.float32),
         cost_estimate=cost(2 * chains * modes * ROWS * LANES, 2 * modes * ROWS * LANES),
+        compiler_params=pltpu.CompilerParams(vmem_limit_bytes=8 * 2**20),
         name="field",
-    )(theta, basis)
+    )(
+        pltpu.with_memory_space_constraint(theta, pltpu.HBM),
+        pltpu.with_memory_space_constraint(basis, pltpu.HBM),
+    )
 
 
 def left_half():
@@ -114,7 +136,6 @@
 
 
 def combine_kernel(
-    place_ref,
     parts_ref,
     mean_ref,
     face_ref,
@@ -152,7 +173,7 @@
     weight = code16(weight_ref[...], UNIT_SPAN)
     near, far = rows_of(pairs_ref[0:1]), rows_of(pairs_ref[1:2])
     code = near * 4 + jnp.where(near == far, 0, far - near - NZ)
-    fault = code16(rows_of(fault_ref[...]), UNIT_SPAN)
+    fault = (rows_of(fault_ref[...]) * 65535.0 + 0.5).astype(jnp.int32) - 32768
     bounds = jnp.broadcast_to(bound, (2, LANES))
     zeros = jnp.zeros((2, LANES), jnp.int32)
     forms = (
@@ -172,22 +193,23 @@
         ],
     )
     forms = [jnp.concatenate(form, 0) for form in forms]
-    fixed = jnp.where(place_ref[1] == 0, forms[0], forms[1])
+    fixed = jnp.where(place()[1] == 0, forms[0], forms[1])
     field = pack(scaled(even), scaled(odd))
     for k in range(out_ref.shape[0]):
         out_ref[k, 0:ROWS] = field
         out_ref[k, ROWS:PIECE] = fixed
 
 
-def combine(place, parts, *fixed):
+def combine(parts, *fixed):
     return pl.pallas_call(
         combine_kernel,
-        in_specs=[SMEM] + [VMEM] * (1 + len(fixed)),
+        in_specs=[VMEM] * (1 + len(fixed)),
         out_specs=VMEM,
         out_shape=jax.ShapeDtypeStruct((LAYERS, PIECE, LANES), jnp.int32),
         cost_estimate=cost(2**17, 2**20),
+        compiler_params=pltpu.CompilerParams(vmem_limit_bytes=4 * 2**20),
         name="combine",
-    )(place, parts, *fixed)
+    )(parts, *fixed)
 
 
 def harmonic(left, right):
@@ -228,7 +250,6 @@
 
 
 def physics_kernel(
-    place_ref,
     own_ref,
     other_ref,
     pressure_ref,
@@ -237,6 +258,7 @@
     coef,
     inverse,
     local,
+    fault,
     weight,
     data,
     resid,
@@ -245,7 +267,7 @@
     dir_a,
     dir_b,
 ):
-    here, core = place_ref[0], place_ref[1]
+    here, core = place()
     zeros = jnp.zeros((ROWS, LANES), jnp.float32)
     for pad in (0, LAYERS + 1):
         for k in range(2):
@@ -264,8 +286,34 @@
     row = lax.broadcasted_iota(jnp.int32, (ROWS, LANES), 0)
     z_inside = (lane & (NZ - 1)) < NZ - 1
     y_inside = row < ROWS - 1
-    keys = lax.broadcasted_iota(jnp.int32, (THROWS * ROWS, LANES), 0)
-    lanes_of = lax.broadcasted_iota(jnp.int32, (LANES, LANES), 0)
+    keys = lax.broadcasted_iota(jnp.int32, (THROWS * ROWS, SLOT_ROWS * LANES), 0)
+    lanes_of = lax.broadcasted_iota(jnp.int32, (LANES, SLOT_ROWS * LANES), 0)
+
+    def join(x):
+        own, other = own_ref[x, PIECE - 4 : PIECE - 2], other_ref[x, PIECE - 4 : PIECE - 2]
+        slots = jnp.where(core == 0, other, own)
+        slots = jnp.concatenate([slots[h : h + 1] for h in range(SLOT_ROWS)], 1)
+        code, amount = high16(slots), low16(slots) + 32768
+        throw, cell = code & 3, code >> 2
+        key = jnp.where(throw > 0, (throw - 1) * ROWS + (cell >> 7), -1)
+        hit = keys == key
+        parts = [
+            jnp.where(hit, part.astype(jnp.float32), 0.0) for part in (amount >> 8, amount & 255)
+        ]
+        rows_hot = jnp.concatenate(parts, 0).astype(jnp.bfloat16)
+        lanes_hot = jnp.where(lanes_of == (cell & (LANES - 1)), 1.0, 0.0).astype(jnp.bfloat16)
+        sums = lax.dot_general(
+            rows_hot, lanes_hot, (((1,), (1,)), ((), ())), preferred_element_type=jnp.float32
+        )
+        count = THROWS * ROWS
+        total = (sums[:count] * 256.0 + sums[count:]) * (1.0 / 65535.0)
+        for s in range(THROWS):
+            even, odd = spread(total[s * ROWS : (s + 1) * ROWS])
+            fault[x, s, 0] = even
+            fault[x, s, 1] = odd
+
+    for x in range(LAYERS):
+        join(x)
 
     def prepare(x, carry):
         own, other = own_ref[x, ROWS:PIECE], other_ref[x, ROWS:PIECE]
@@ -281,21 +329,6 @@
         obs_data = spread(value16(low16(second[0:16]), WELL_SPAN))
         halves = (high16(second[16:24]), low16(second[16:24]))
         obs_weight = spread(value16(jnp.concatenate(halves, 0), UNIT_SPAN))
-        slots = second[28:30]
-        faults = jnp.zeros((THROWS * ROWS, LANES), jnp.float32)
-        for h in range(SLOT_ROWS):
-            code = high16(slots[h : h + 1])
-            throw, cell = code & 3, code >> 2
-            key = jnp.where(throw > 0, (throw - 1) * ROWS + (cell >> 7), -1)
-            amount = value16(low16(slots[h : h + 1]), UNIT_SPAN)
-            rows_hot = jnp.where(keys == key, amount, 0.0)
-            lanes_hot = jnp.where(lanes_of == (cell & (LANES - 1)), 1.0, 0.0).astype(jnp.bfloat16)
-            for _ in range(3):
-                piece = rows_hot.astype(jnp.bfloat16)
-                faults = faults + lax.dot_general(
-                    piece, lanes_hot, (((1,), (1,)), ((), ())), preferred_element_type=jnp.float32
-                )
-                rows_hot = rows_hot - piece.astype(jnp.float32)
         even, odd = perm[x + 1, 0], perm[x + 1, 1]
         inside = jnp.where(x < LAYERS - 1, 1.0, 0.0)
         xp_even = harmonic(even, perm[x + 2, 0]) * mult_x[0] * inside
@@ -309,9 +342,8 @@
         to_odd = [xp_odd, xm_odd, zp_odd, behind(zp_odd, 1), y_odd, y_even]
         back_even, back_odd = [], []
         for s in range(1, THROWS + 1):
-            fault = spread(faults[(s - 1) * ROWS : s * ROWS])
-            fault_even = harmonic(even, ahead(odd, s)) * fault[0]
-            fault_odd = harmonic(odd, up(ahead(even, s))) * fault[1]
+            fault_even = harmonic(even, ahead(odd, s)) * fault[x, s - 1, 0]
+            fault_odd = harmonic(odd, up(ahead(even, s))) * fault[x, s - 1, 1]
             to_even.append(fault_even)
             to_odd.append(fault_odd)
             back_even.append(down(behind(fault_odd, s)))
@@ -346,7 +378,7 @@
             field[x + 1, side] = zeros
         return xp_even, xp_odd
 
-    lax.fori_loop(0, LAYERS, prepare, (zeros, zeros))
+    lax.fori_loop(0, LAYERS, prepare, (zeros, zeros), unroll=4)
 
     def sweep(total, source_dir, target_dir, keep, gain):
         for x in range(LAYERS):
@@ -443,7 +475,7 @@
         glogk_ref[m, 1] = second
 
 
-def physics(place, own, other, copies):
+def physics(own, other, copies):
     f32 = jnp.float32
 
     def buffer(*lead):
@@ -452,7 +484,7 @@
     padded = LAYERS + 2
     return pl.pallas_call(
         physics_kernel,
-        in_specs=[SMEM] + [VMEM] * 2,
+        in_specs=[VMEM] * 2,
         out_specs=[VMEM, VMEM],
         out_shape=[
             jax.ShapeDtypeStruct((2, ROWS, LANES), f32),
@@ -463,6 +495,7 @@
             buffer(LAYERS, 12, 2),
             buffer(LAYERS, 2),
             buffer(12, 2),
+            buffer(LAYERS, THROWS, 2),
             buffer(LAYERS, 2),
             buffer(LAYERS, 2),
             buffer(LAYERS, 2),
@@ -471,10 +504,10 @@
             buffer(padded, 2),
             buffer(padded, 2),
         ],
-        compiler_params=pltpu.CompilerParams(vmem_limit_bytes=24 * 2**20),
+        compiler_params=pltpu.CompilerParams(vmem_limit_bytes=12 * 2**20),
         cost_estimate=cost(2**32, 2**24),
         name="physics",
-    )(place, own, other)
+    )(own, other)
 
 
 def gradient_kernel(glogk_ref, basis_ref, out_ref, rows):
@@ -488,10 +521,8 @@
             basis_ref[row * LANES : (row + 1) * LANES, :],
             preferred_element_type=jnp.float32,
         )
-        if row == 0:
-            out_ref[...] = part
-        else:
-            out_ref[...] += part
+        total = part if row == 0 else total + part
+    out_ref[...] = total.astype(jnp.bfloat16)
 
 
 def gradient_of(glogk, basis):
@@ -500,16 +531,17 @@
         gradient_kernel,
         in_specs=[VMEM, VMEM],
         out_specs=VMEM,
-        out_shape=jax.ShapeDtypeStruct((chains, basis.shape[1]), jnp.float32),
+        out_shape=jax.ShapeDtypeStruct((chains, basis.shape[1]), jnp.bfloat16),
         scratch_shapes=[pltpu.VMEM((chains, ROWS, LANES), jnp.float32)],
-        compiler_params=pltpu.CompilerParams(vmem_limit_bytes=16 * 2**20),
+        compiler_params=pltpu.CompilerParams(vmem_limit_bytes=6 * 2**20),
         cost_estimate=cost(2 * chains * basis.size, 2 * basis.size),
         name="gradient",
     )(glogk, basis)
 
 
 def copies_kernel(one_ref, two_ref, out_ref):
-    total = (one_ref[...] + two_ref[...]).astype(jnp.bfloat16)
+    total = one_ref[...].astype(jnp.float32) + two_ref[...].astype(jnp.float32)
+    total = total.astype(jnp.bfloat16)
     for k in range(out_ref.shape[0]):
         out_ref[k] = total
 
@@ -521,6 +553,7 @@
         out_specs=VMEM,
         out_shape=jax.ShapeDtypeStruct((count, *one.shape), jnp.bfloat16),
         cost_estimate=cost(2**16, 2**19),
+        compiler_params=pltpu.CompilerParams(vmem_limit_bytes=4 * 2**20),
         name="copies",
     )(one, two)
 
@@ -544,14 +577,10 @@
 ):
     modes_n, cells_n = lax.axis_size("modes"), lax.axis_size("cells")
     size = cells_n * modes_n
-    here = lax.axis_index("cells")
-    core = lax.axis_index("modes") & 1
-    place = jnp.stack([here, core]).astype(jnp.int32)
 
     partial_field = field_of(theta.T, basis).reshape(modes_n, 2, ROWS, LANES)
     parts = lax.all_to_all(partial_field, "modes", 0, 0)
     pieces = combine(
-        place,
         parts,
         mean_logk.reshape(ROWS, LANES),
         face_mult,
@@ -564,7 +593,7 @@
     )
     pieces = lax.all_to_all(pieces, "cells", 0, 0)
     others = exchange(pieces, 1, size)
-    pressure, glogk = physics(place, pieces, others, modes_n)
+    pressure, glogk = physics(pieces, others, modes_n)
     glogk = lax.all_to_all(glogk, "modes", 0, 0)
     grad_rows = gradient_of(glogk, basis)
     half = cells_n // 2

time: 94.1 us -> 83.8 us (0.89)
  blocking collectives: 34.6 us -> 46.5 us
  Pallas kernels: 20.4 us -> 13.2 us
  waiting for transfers between devices: 23.2 us -> 17 us
  starting transfers between devices: 10.4 us -> 4.66 us
  local copies, waits for them, and re-layouts: 2.62 us -> 0.67 us
    all_to_all x0 -> x1, blocking collectives: none -> 12.1 us  [body(): parts = lax.all_to_all(partial_field, 'modes', 0, 0)]
    pallas_call x3, Pallas kernels: 18.4 us -> 12.1 us  [the longest x1 9.49 us: physics(): pl.pallas_call(physics_kernel, in_specs=[VMEM] * 2, out_specs=[VMEM, VMEM...]
    all_to_all x1 -> x0, waiting for transfers between devices: 5.92 us -> none  [body(): parts = lax.all_to_all(partial_field, 'modes', 0, 0)]
    all_to_all x1 -> x0, starting transfers between devices: 5.78 us -> none  [body(): parts = lax.all_to_all(partial_field, 'modes', 0, 0)]
    unnamed x17 -> x25, local copies, waits for them, and re-layouts: 2.62 us -> 0.67 us
  transfers between devices with their start and end apart: 4 -> 3, of which waited for: 4 -> 3; matrix products, arithmetic and copies ran while one was open for 1% -> 1% of each run, Pallas kernels for 0% -> 0%
where the time goes in v2:
time: 83.8 us; the launch traced here: 83.5 us
  blocking collectives  46.5 us (55%)
  waiting for transfers between devices  17 us (20%)
  Pallas kernels  13.2 us (16%)
  starting transfers between devices  4.66 us (6%)
    all_to_all x1, blocking collectives, body(): pieces = lax.all_to_all(pieces, 'cells', 0, 0)  24.6 us
    all_to_all x1, blocking collectives, body(): parts = lax.all_to_all(partial_field, 'modes', 0, 0)  12.1 us
    all_to_all x1, waiting for transfers between devices, body(): lax.all_to_all(grad_rows, 'cells', 0, 0, axis_index_groups=groups)  10.4 us
    all_to_all x1, blocking collectives, body(): glogk = lax.all_to_all(glogk, 'modes', 0, 0)  9.79 us
    pallas_call x1, Pallas kernels, physics(): pl.pallas_call(physics_kernel, in_specs=[VMEM] * 2, out_specs=[VMEM, VMEM...  9.49 us
    ppermute x2, waiting for transfers between devices, exchange(): return lax.ppermute(value, AXES, [(i, i ^ mask) for i in range(size)])  6.52 us
    all_to_all x1, starting transfers between devices, body(): lax.all_to_all(grad_rows, 'cells', 0, 0, axis_index_groups=groups)  4.03 us
    pallas_call x1, Pallas kernels, field_of(): pl.pallas_call(field_kernel, in_specs=[pl.BlockSpec(memory_space=pltpu.HB...  2.35 us
  transfers between devices with their start and end apart: 3, of which 3 were waited for; matrix products, arithmetic and copies ran while one was open for 1% of the time, Pallas kernels for 0%

profile of v2, /device:TPU:8, one launch (start us, length us, event | category | flops | bytes accessed | tf_op | source)
XLA Modules:
  0.0 83.5 jit_solution(16055952637654864143)
XLA Ops:
  0.6 0.0 copy-start.8
  0.6 0.0 copy-start.7
  0.7 0.0 copy-start.6
  0.7 0.0 copy-start.5
  0.7 0.0 copy-start.4
  0.7 0.0 copy-start.3
  0.7 0.0 copy-start.1
  0.7 0.0 copy-start.2
  0.7 2.4 %field.1 = f32[32,16,128]{2,1,0:T(8,128)S(1)} custom-call(f32[32,512]{1,0:T(8,128)} %bitcast.24, bf16[2048,512]{1,0:T(8,128)(2,1)} %basis_ref.1), custom_call_target="tpu_custom_call" | custom-call | flops 67108864 | bytes 2097152 | tf_op jit(solution)/shard_map/field/pallas_call | solution.py:77
  3.1 12.1 %all_to_all.20.parts_ref = f32[16,2,16,128]{3,2,1,0:T(8,128)S(1)} all-to-all(f32[16,2,16,128]{3,2,1,0:T(8,128)S(1)} %bitcast.15), channel_id=1, replica_groups=mesh['cells'=16,'modes'=16] {'modes'}, dimensions={0} | all-to-all | bytes 524288 | tf_op jit(solution)/shard_map/all_to_all | solution.py:582
  15.2 0.0 copy-done.8
  15.2 0.0 copy-done.7
  15.2 0.0 copy-done.6
  15.2 0.0 copy-done.5
  15.2 0.2 combine.1
  15.5 24.6 %all_to_all.21.own_ref = s32[16,48,128]{2,1,0:T(8,128)S(1)} all-to-all(s32[16,48,128]{2,1,0:T(8,128)S(1)} %combine.1), channel_id=1, replica_groups=mesh['cells'=16,'modes'=16] {'cells'}, dimensions={0} | all-to-all | bytes 786432 | tf_op jit(solution)/shard_map/all_to_all | solution.py:594
  40.0 0.0 collective-permute-start
  40.0 1.7 %collective-permute-done.other_ref = s32[16,48,128]{2,1,0:T(8,128)S(1)} collective-permute-done((s32[16,48,128]{2,1,0:T(8,128)S(1)}, s32[16,48,128]{2,1,0:T(8,128)S(1)}, u32[]{:S(2)}, u32[]{:S(2)}) %collective-permute-start) | collective-permute-done | bytes 393248 | tf_op jit(solution)/shard_map/ppermute | solution.py:562
  41.8 9.5 %physics.1 = (f32[2,16,128]{2,1,0:T(8,128)S(1)}, bf16[16,2,16,128]{3,2,1,0:T(8,128)(2,1)S(1)}) custom-call(s32[16,48,128]{2,1,0:T(8,128)S(1)} %all_to_all.21.own_ref, s32[16,48,128]{2,1,0:T(8,128)S(1)} %collective-permute-done.other_ref), custom_call_target="tpu_custom_call" | custom-call | flops 4294967296 | bytes 16777216 | tf_op jit(solution)/shard_map/physics/pallas_call | solution.py:485
  51.3 0.0 copy-start.9
  51.3 0.0 copy-start.11
  51.3 9.8 %all_to_all.22.glogk_ref = bf16[16,2,16,128]{3,2,1,0:T(8,128)(2,1)S(1)} all-to-all(bf16[16,2,16,128]{3,2,1,0:T(8,128)(2,1)S(1)} %get-tuple-element.5), channel_id=1, replica_groups=mesh['cells'=16,'modes'=16] {'modes'}, dimensions={0} | all-to-all | bytes 262144 | tf_op jit(solution)/shard_map/all_to_all | solution.py:597
  61.1 0.0 copy-done
  61.1 0.4 gradient.1.one_ref
  61.5 0.6 collective-permute-start.1
  62.1 4.8 %collective-permute-done.1.two_ref = bf16[32,512]{1,0:T(8,128)(2,1)S(1)} collective-permute-done((bf16[32,512]{1,0:T(8,128)(2,1)S(1)}, bf16[32,512]{1,0:T(8,128)(2,1)S(1)}, u32[]{:S(2)}, u32[]{:S(2)}) %collective-permute-start.1) | collective-permute-done | bytes 32800 | tf_op jit(solution)/shard_map/ppermute | solution.py:562
  66.9 0.7 copies.1
  67.6 4.0 %all-to-all-start.3 = ((bf16[8,32,512]{2,1,0:T(8,128)(2,1)}), bf16[8,32,512]{2,1,0:T(8,128)(2,1)S(1)}, u32[]{:S(2)}, u32[]{:S(2)}) async-start(bf16[8,32,512]{2,1,0:T(8,128)(2,1)} %copies.1), calls=%async_computation.3 | async-start | bytes 524288 | tf_op jit(solution)/shard_map/all_to_all | solution.py:602
  71.7 0.6 copy.16
  72.3 10.4 %all-to-all-done.3 = bf16[8,32,512]{2,1,0:T(8,128)(2,1)S(1)} async-done(((bf16[8,32,512]{2,1,0:T(8,128)(2,1)}), bf16[8,32,512]{2,1,0:T(8,128)(2,1)S(1)}, u32[]{:S(2)}, u32[]{:S(2)}) %all-to-all-start.3) | async-done | bytes 262176 | tf_op jit(solution)/shard_map/all_to_all | solution.py:602
  82.8 0.0 copy-start.10
  82.8 0.7 multiply_add_fusion
  (9 shorter events, 0.1 us)
Async XLA Ops:
  0.6 14.5 %copy-start.8 = (f32[256]{0:T(256)S(1)}, f32[256]{0:T(256)}, u32[]{:S(2)}) copy-start(f32[256]{0:T(256)} %param.20) | copy-start | bytes 3076
  0.6 14.5 %copy-start.7 = (s32[256,2]{0,1:T(2,128)S(1)}, s32[256,2]{0,1:T(2,128)}, u32[]{:S(2)}) copy-start(s32[256,2]{0,1:T(2,128)} %param.19) | copy-start | bytes 6148
  0.7 14.5 %copy-start.6 = (f32[2048]{0:T(1024)S(1)}, f32[2048]{0:T(1024)}, u32[]{:S(2)}) copy-start(f32[2048]{0:T(1024)} %param.18) | copy-start | bytes 24580
  0.7 14.5 %copy-start.5 = (f32[2048]{0:T(1024)S(1)}, f32[2048]{0:T(1024)}, u32[]{:S(2)}) copy-start(f32[2048]{0:T(1024)} %param.17) | copy-start | bytes 24580
  0.7 14.5 %copy-start.4 = (f32[2048]{0:T(1024)S(1)}, f32[2048]{0:T(1024)}, u32[]{:S(2)}) copy-start(f32[2048]{0:T(1024)} %param.16) | copy-start | bytes 24580
  0.7 14.5 %copy-start.3 = (f32[2048]{0:T(1024)S(1)}, f32[2048]{0:T(1024)}, u32[]{:S(2)}) copy-start(f32[2048]{0:T(1024)} %param.15) | copy-start | bytes 24580
  0.7 14.5 %copy-start.1 = (f32[3,2048]{1,0:T(4,128)S(1)}, f32[3,2048]{1,0:T(4,128)}, u32[]{:S(2)}) copy-start(f32[3,2048]{1,0:T(4,128)} %face_ref.1) | copy-start | bytes 73732
  0.7 14.5 %copy-start.2 = (f32[2048]{0:T(1024)S(1)}, f32[2048]{0:T(1024)}, u32[]{:S(2)}) copy-start(f32[2048]{0:T(1024)} %param.13) | copy-start | bytes 24580
  40.0 21.0 %copy-start = (bf16[2048,512]{1,0:T(8,128)(2,1)S(1)}, bf16[2048,512]{1,0:T(8,128)(2,1)}, u32[]{:S(2)}) copy-start(bf16[2048,512]{1,0:T(8,128)(2,1)} %basis_ref.1) | copy-start | bytes 6291460
  40.0 1.7 %collective-permute-start = (s32[16,48,128]{2,1,0:T(8,128)S(1)}, s32[16,48,128]{2,1,0:T(8,128)S(1)}, u32[]{:S(2)}, u32[]{:S(2)}) collective-permute-start(s32[16,48,128]{2,1,0:T(8,128)S(1)} %all_to_all.21.own_ref), channel_id=1, source_target_pairs={{0,1},{1,0},{2,3},{3,2},{4,5},{5,4},{6,7},{7,6},{8,9},{9,8},{10,11... | collective-permute-start | bytes 1179656 | tf_op jit(solution)/shard_map/ppermute | solution.py:562
  51.3 31.5 %copy-start.9 = (f32[512,32]{0,1:T(8,128)S(1)}, f32[512,32]{0,1:T(8,128)}, u32[]{:S(2)}) copy-start(f32[512,32]{0,1:T(8,128)} %param.11) | copy-start | bytes 196612
  51.3 31.5 %copy-start.11 = (f32[512,32]{0,1:T(8,128)S(1)}, f32[512,32]{0,1:T(8,128)}, u32[]{:S(2)}) copy-start(f32[512,32]{0,1:T(8,128)} %param.21) | copy-start | bytes 196612
  61.5 5.4 %collective-permute-start.1 = (bf16[32,512]{1,0:T(8,128)(2,1)S(1)}, bf16[32,512]{1,0:T(8,128)(2,1)S(1)}, u32[]{:S(2)}, u32[]{:S(2)}) collective-permute-start(bf16[32,512]{1,0:T(8,128)(2,1)S(1)} %gradient.1.one_ref), channel_id=1, source_target_pairs={{0,128},{1,129},{2,130},{3,131},{4,132},{5,133},{6,134},{7,135},{8... | collective-permute-start | bytes 98312 | tf_op jit(solution)/shard_map/ppermute | solution.py:562
  67.6 15.1 %all-to-all-start.3 = ((bf16[8,32,512]{2,1,0:T(8,128)(2,1)}), bf16[8,32,512]{2,1,0:T(8,128)(2,1)S(1)}, u32[]{:S(2)}, u32[]{:S(2)}) async-start(bf16[8,32,512]{2,1,0:T(8,128)(2,1)} %copies.1), calls=%async_computation.3 | async-start | bytes 524288 | tf_op jit(solution)/shard_map/all_to_all | solution.py:602
  82.8 0.7 copy-start.10

commit v3 on v2

--- a/solution.py
+++ b/solution.py
@@ -73,7 +73,7 @@
 
 def field_of(theta, basis):
     chains, modes = theta.shape
-    steps = 4
+    steps = 2
     return pl.pallas_call(
         field_kernel,
         in_specs=[pl.BlockSpec(memory_space=pltpu.HBM)] * 2,
@@ -380,8 +380,9 @@
 
     lax.fori_loop(0, LAYERS, prepare, (zeros, zeros), unroll=4)
 
-    def sweep(total, source_dir, target_dir, keep, gain):
-        for x in range(LAYERS):
+    def sweep(total, source_dir, target_dir, keep, gain, base=0, count=LAYERS):
+        for step in range(count):
+            x = base + step
             even, odd = source_dir[x + 1, 0], source_dir[x + 1, 1]
             c = lambda k, side: coef[x, k, side]
             acc_even = c(0, 0) * source_dir[x + 2, 0] + c(1, 0) * source_dir[x, 0]
@@ -432,7 +433,12 @@
             resid[x, side] = start
             dir_a[x + 1, side] = start * (1.0 / CENTER)
             adjoint[x + 1, side] = zeros
-    solve(adjoint)
+    for k in range(SWEEPS):
+        reach = SWEEPS - k
+        count = min(2 * reach + 1, LAYERS)
+        base = jnp.clip(here - reach, 0, LAYERS - count)
+        pair = (dir_a, dir_b) if k % 2 == 0 else (dir_b, dir_a)
+        sweep(adjoint, *pair, *FACTORS[k], base, count)
 
     def around(ref, extra=None):
         def read(layer):

time: 83.8 us -> 82.6 us (0.986)
  Pallas kernels: 13.2 us -> 12 us
    pallas_call x1, Pallas kernels: 9.49 us -> 8.36 us  [physics(): pl.pallas_call(physics_kernel, in_specs=[VMEM] * 2, out_specs=[VMEM, VMEM...]
where the time goes in v3:
time: 82.6 us; the launch traced here: 82.2 us
  blocking collectives  46.4 us (56%)
  waiting for transfers between devices  17 us (21%)
  Pallas kernels  12 us (15%)
  starting transfers between devices  4.67 us (6%)
    all_to_all x1, blocking collectives, body(): pieces = lax.all_to_all(pieces, 'cells', 0, 0)  24.6 us
    all_to_all x1, blocking collectives, body(): parts = lax.all_to_all(partial_field, 'modes', 0, 0)  12.1 us
    all_to_all x1, waiting for transfers between devices, body(): lax.all_to_all(grad_rows, 'cells', 0, 0, axis_index_groups=groups)  10.4 us
    all_to_all x1, blocking collectives, body(): glogk = lax.all_to_all(glogk, 'modes', 0, 0)  9.78 us
    pallas_call x1, Pallas kernels, physics(): pl.pallas_call(physics_kernel, in_specs=[VMEM] * 2, out_specs=[VMEM, VMEM...  8.36 us
    ppermute x2, waiting for transfers between devices, exchange(): return lax.ppermute(value, AXES, [(i, i ^ mask) for i in range(size)])  6.52 us
    all_to_all x1, starting transfers between devices, body(): lax.all_to_all(grad_rows, 'cells', 0, 0, axis_index_groups=groups)  4.04 us
    pallas_call x1, Pallas kernels, field_of(): pl.pallas_call(field_kernel, in_specs=[pl.BlockSpec(memory_space=pltpu.HB...  2.24 us
  transfers between devices with their start and end apart: 3, of which 3 were waited for; matrix products, arithmetic and copies ran while one was open for 1% of the time, Pallas kernels for 0%

profile of v3, /device:TPU:8, one launch (start us, length us, event | category | flops | bytes accessed | tf_op | source)
XLA Modules:
  0.0 82.2 jit_solution(7900243382387768289)
XLA Ops:
  0.6 0.0 copy-start.8
  0.6 0.0 copy-start.7
  0.7 0.0 copy-start.6
  0.7 0.0 copy-start.5
  0.7 0.0 copy-start.4
  0.7 0.0 copy-start.3
  0.7 0.0 copy-start.1
  0.7 0.0 copy-start.2
  0.7 2.2 %field.1 = f32[32,16,128]{2,1,0:T(8,128)S(1)} custom-call(f32[32,512]{1,0:T(8,128)} %bitcast.24, bf16[2048,512]{1,0:T(8,128)(2,1)} %basis_ref.1), custom_call_target="tpu_custom_call" | custom-call | flops 67108864 | bytes 2097152 | tf_op jit(solution)/shard_map/field/pallas_call | solution.py:77
  3.0 12.1 %all_to_all.20.parts_ref = f32[16,2,16,128]{3,2,1,0:T(8,128)S(1)} all-to-all(f32[16,2,16,128]{3,2,1,0:T(8,128)S(1)} %bitcast.15), channel_id=1, replica_groups=mesh['cells'=16,'modes'=16] {'modes'}, dimensions={0} | all-to-all | bytes 524288 | tf_op jit(solution)/shard_map/all_to_all | solution.py:588
  15.0 0.0 copy-done.8
  15.0 0.0 copy-done.7
  15.0 0.0 copy-done.6
  15.1 0.2 combine.1
  15.3 24.6 %all_to_all.21.own_ref = s32[16,48,128]{2,1,0:T(8,128)S(1)} all-to-all(s32[16,48,128]{2,1,0:T(8,128)S(1)} %combine.1), channel_id=1, replica_groups=mesh['cells'=16,'modes'=16] {'cells'}, dimensions={0} | all-to-all | bytes 786432 | tf_op jit(solution)/shard_map/all_to_all | solution.py:600
  39.9 0.0 collective-permute-start
  39.9 1.7 %collective-permute-done.other_ref = s32[16,48,128]{2,1,0:T(8,128)S(1)} collective-permute-done((s32[16,48,128]{2,1,0:T(8,128)S(1)}, s32[16,48,128]{2,1,0:T(8,128)S(1)}, u32[]{:S(2)}, u32[]{:S(2)}) %collective-permute-start) | collective-permute-done | bytes 393248 | tf_op jit(solution)/shard_map/ppermute | solution.py:568
  41.7 8.4 %physics.1 = (f32[2,16,128]{2,1,0:T(8,128)S(1)}, bf16[16,2,16,128]{3,2,1,0:T(8,128)(2,1)S(1)}) custom-call(s32[16,48,128]{2,1,0:T(8,128)S(1)} %all_to_all.21.own_ref, s32[16,48,128]{2,1,0:T(8,128)S(1)} %collective-permute-done.other_ref), custom_call_target="tpu_custom_call" | custom-call | flops 4294967296 | bytes 16777216 | tf_op jit(solution)/shard_map/physics/pallas_call | solution.py:491
  50.0 0.0 copy-start.9
  50.0 0.0 copy-start.11
  50.0 9.8 %all_to_all.22.glogk_ref = bf16[16,2,16,128]{3,2,1,0:T(8,128)(2,1)S(1)} all-to-all(bf16[16,2,16,128]{3,2,1,0:T(8,128)(2,1)S(1)} %get-tuple-element.5), channel_id=1, replica_groups=mesh['cells'=16,'modes'=16] {'modes'}, dimensions={0} | all-to-all | bytes 262144 | tf_op jit(solution)/shard_map/all_to_all | solution.py:603
  59.8 0.4 gradient.1.one_ref
  60.2 0.6 collective-permute-start.1
  60.9 4.8 %collective-permute-done.1.two_ref = bf16[32,512]{1,0:T(8,128)(2,1)S(1)} collective-permute-done((bf16[32,512]{1,0:T(8,128)(2,1)S(1)}, bf16[32,512]{1,0:T(8,128)(2,1)S(1)}, u32[]{:S(2)}, u32[]{:S(2)}) %collective-permute-start.1) | collective-permute-done | bytes 32800 | tf_op jit(solution)/shard_map/ppermute | solution.py:568
  65.7 0.7 copies.1
  66.4 4.0 %all-to-all-start.3 = ((bf16[8,32,512]{2,1,0:T(8,128)(2,1)}), bf16[8,32,512]{2,1,0:T(8,128)(2,1)S(1)}, u32[]{:S(2)}, u32[]{:S(2)}) async-start(bf16[8,32,512]{2,1,0:T(8,128)(2,1)} %copies.1), calls=%async_computation.3 | async-start | bytes 524288 | tf_op jit(solution)/shard_map/all_to_all | solution.py:608
  70.4 0.6 copy.16
  71.0 10.4 %all-to-all-done.3 = bf16[8,32,512]{2,1,0:T(8,128)(2,1)S(1)} async-done(((bf16[8,32,512]{2,1,0:T(8,128)(2,1)}), bf16[8,32,512]{2,1,0:T(8,128)(2,1)S(1)}, u32[]{:S(2)}, u32[]{:S(2)}) %all-to-all-start.3) | async-done | bytes 262176 | tf_op jit(solution)/shard_map/all_to_all | solution.py:608
  81.5 0.0 copy-done.9
  81.5 0.0 copy-done.11
  81.6 0.0 copy-start.10
  81.6 0.7 multiply_add_fusion
  (9 shorter events, 0.1 us)
Async XLA Ops:
  0.6 14.4 %copy-start.8 = (f32[256]{0:T(256)S(1)}, f32[256]{0:T(256)}, u32[]{:S(2)}) copy-start(f32[256]{0:T(256)} %param.20) | copy-start | bytes 3076
  0.6 14.4 %copy-start.7 = (s32[256,2]{0,1:T(2,128)S(1)}, s32[256,2]{0,1:T(2,128)}, u32[]{:S(2)}) copy-start(s32[256,2]{0,1:T(2,128)} %param.19) | copy-start | bytes 6148
  0.7 14.4 %copy-start.6 = (f32[2048]{0:T(1024)S(1)}, f32[2048]{0:T(1024)}, u32[]{:S(2)}) copy-start(f32[2048]{0:T(1024)} %param.18) | copy-start | bytes 24580
  0.7 14.4 %copy-start.5 = (f32[2048]{0:T(1024)S(1)}, f32[2048]{0:T(1024)}, u32[]{:S(2)}) copy-start(f32[2048]{0:T(1024)} %param.17) | copy-start | bytes 24580
  0.7 14.4 %copy-start.4 = (f32[2048]{0:T(1024)S(1)}, f32[2048]{0:T(1024)}, u32[]{:S(2)}) copy-start(f32[2048]{0:T(1024)} %param.16) | copy-start | bytes 24580
  0.7 14.4 %copy-start.3 = (f32[2048]{0:T(1024)S(1)}, f32[2048]{0:T(1024)}, u32[]{:S(2)}) copy-start(f32[2048]{0:T(1024)} %param.15) | copy-start | bytes 24580
  0.7 14.4 %copy-start.1 = (f32[3,2048]{1,0:T(4,128)S(1)}, f32[3,2048]{1,0:T(4,128)}, u32[]{:S(2)}) copy-start(f32[3,2048]{1,0:T(4,128)} %face_ref.1) | copy-start | bytes 73732
  0.7 14.4 %copy-start.2 = (f32[2048]{0:T(1024)S(1)}, f32[2048]{0:T(1024)}, u32[]{:S(2)}) copy-start(f32[2048]{0:T(1024)} %param.13) | copy-start | bytes 24580
  39.9 19.9 %copy-start = (bf16[2048,512]{1,0:T(8,128)(2,1)S(1)}, bf16[2048,512]{1,0:T(8,128)(2,1)}, u32[]{:S(2)}) copy-start(bf16[2048,512]{1,0:T(8,128)(2,1)} %basis_ref.1) | copy-start | bytes 6291460
  39.9 1.7 %collective-permute-start = (s32[16,48,128]{2,1,0:T(8,128)S(1)}, s32[16,48,128]{2,1,0:T(8,128)S(1)}, u32[]{:S(2)}, u32[]{:S(2)}) collective-permute-start(s32[16,48,128]{2,1,0:T(8,128)S(1)} %all_to_all.21.own_ref), channel_id=1, source_target_pairs={{0,1},{1,0},{2,3},{3,2},{4,5},{5,4},{6,7},{7,6},{8,9},{9,8},{10,11... | collective-permute-start | bytes 1179656 | tf_op jit(solution)/shard_map/ppermute | solution.py:568
  50.0 31.5 %copy-start.9 = (f32[512,32]{0,1:T(8,128)S(1)}, f32[512,32]{0,1:T(8,128)}, u32[]{:S(2)}) copy-start(f32[512,32]{0,1:T(8,128)} %param.11) | copy-start | bytes 196612
  50.0 31.5 %copy-start.11 = (f32[512,32]{0,1:T(8,128)S(1)}, f32[512,32]{0,1:T(8,128)}, u32[]{:S(2)}) copy-start(f32[512,32]{0,1:T(8,128)} %param.21) | copy-start | bytes 196612
  60.2 5.4 %collective-permute-start.1 = (bf16[32,512]{1,0:T(8,128)(2,1)S(1)}, bf16[32,512]{1,0:T(8,128)(2,1)S(1)}, u32[]{:S(2)}, u32[]{:S(2)}) collective-permute-start(bf16[32,512]{1,0:T(8,128)(2,1)S(1)} %gradient.1.one_ref), channel_id=1, source_target_pairs={{0,128},{1,129},{2,130},{3,131},{4,132},{5,133},{6,134},{7,135},{8... | collective-permute-start | bytes 98312 | tf_op jit(solution)/shard_map/ppermute | solution.py:568
  66.4 15.1 %all-to-all-start.3 = ((bf16[8,32,512]{2,1,0:T(8,128)(2,1)}), bf16[8,32,512]{2,1,0:T(8,128)(2,1)S(1)}, u32[]{:S(2)}, u32[]{:S(2)}) async-start(bf16[8,32,512]{2,1,0:T(8,128)(2,1)} %copies.1), calls=%async_computation.3 | async-start | bytes 524288 | tf_op jit(solution)/shard_map/all_to_all | solution.py:608
  81.6 0.7 copy-start.10

commit v4 on v3

--- a/solution.py
+++ b/solution.py
@@ -26,6 +26,10 @@
 
 def place():
     return lax.axis_index("cells"), lax.axis_index("modes") & 1
+
+
+def turn(mode):
+    return 4 * (mode & 1) + 2 * (mode >> 1)
 
 
 def cost(flops, bytes_accessed):
@@ -268,6 +272,15 @@
     dir_b,
 ):
     here, core = place()
+    mode = lax.axis_index("modes")
+    own_turn, other_turn = turn(mode), turn(mode ^ 1)
+
+    def own_at(x):
+        return (x - own_turn) & (LAYERS - 1)
+
+    def other_at(x):
+        return (x - other_turn) & (LAYERS - 1)
+
     zeros = jnp.zeros((ROWS, LANES), jnp.float32)
     for pad in (0, LAYERS + 1):
         for k in range(2):
@@ -277,8 +290,8 @@
             dir_a[pad, k] = zeros
             dir_b[pad, k] = zeros
     for x in range(LAYERS):
-        word = own_ref[x, 0:ROWS]
-        factor = own_ref[x, PIECE - 1 : PIECE].astype(jnp.float32) * (1.0 / (32767.0 * 256.0))
+        word = own_ref[own_at(x), 0:ROWS]
+        factor = own_ref[own_at(x), PIECE - 1 : PIECE].astype(jnp.float32) * (1.0 / (32767.0 * 256.0))
         perm[x + 1, 0] = jnp.exp(high16(word).astype(jnp.float32) * factor)
         perm[x + 1, 1] = jnp.exp(low16(word).astype(jnp.float32) * factor)
 
@@ -290,7 +303,8 @@
     lanes_of = lax.broadcasted_iota(jnp.int32, (LANES, SLOT_ROWS * LANES), 0)
 
     def join(x):
-        own, other = own_ref[x, PIECE - 4 : PIECE - 2], other_ref[x, PIECE - 4 : PIECE - 2]
+        own = own_ref[own_at(x), PIECE - 4 : PIECE - 2]
+        other = other_ref[other_at(x), PIECE - 4 : PIECE - 2]
         slots = jnp.where(core == 0, other, own)
         slots = jnp.concatenate([slots[h : h + 1] for h in range(SLOT_ROWS)], 1)
         code, amount = high16(slots), low16(slots) + 32768
@@ -316,7 +330,7 @@
         join(x)
 
     def prepare(x, carry):
-        own, other = own_ref[x, ROWS:PIECE], other_ref[x, ROWS:PIECE]
+        own, other = own_ref[own_at(x), ROWS:PIECE], other_ref[other_at(x), ROWS:PIECE]
         first = jnp.where(core == 0, own, other)
         second = jnp.where(core == 0, other, own)
         mult_x = spread(value16(high16(first[0:16]), MULT_SPAN))
@@ -597,15 +611,22 @@
         fault_pairs.T,
         fault_mult.reshape(1, SLOT_ROWS * LANES),
     )
-    pieces = lax.all_to_all(pieces, "cells", 0, 0)
+    groups = [
+        [(r + turn(m)) % cells_n * modes_n + m for r in range(cells_n)] for m in range(modes_n)
+    ]
+    pieces = lax.all_to_all(pieces, AXES, 0, 0, axis_index_groups=groups)
     others = exchange(pieces, 1, size)
     pressure, glogk = physics(pieces, others, modes_n)
     glogk = lax.all_to_all(glogk, "modes", 0, 0)
     grad_rows = gradient_of(glogk, basis)
     half = cells_n // 2
     grad_rows = copies_of(grad_rows, exchange(grad_rows, half * modes_n, size), half)
-    groups = [list(range(half)), list(range(half, cells_n))]
-    grad_rows = lax.all_to_all(grad_rows, "cells", 0, 0, axis_index_groups=groups)
+    groups = [
+        [(side + (r + turn(m)) % half) * modes_n + m for r in range(half)]
+        for m in range(modes_n)
+        for side in (0, half)
+    ]
+    grad_rows = lax.all_to_all(grad_rows, AXES, 0, 0, axis_index_groups=groups)
     grad = jnp.sum(grad_rows.astype(jnp.float32), 0).T
     theta_next = theta - STEP_SIZE * (grad + theta) + math.sqrt(2.0 * STEP_SIZE) * noise
     return (theta_next, grad, pressure.reshape(2, NY * NZ))

time: 82.6 us -> 82 us (level)
  starting transfers between devices: 4.67 us -> 6.55 us
  waiting for transfers between devices: 17 us -> 15.5 us
  blocking collectives: 46.4 us -> 45.4 us
    all_to_all x1, blocking collectives: 24.6 us -> 22.2 us  [body(): pieces = lax.all_to_all(pieces, AXES, 0, 0, axis_index_groups=groups)]
    all_to_all x1, blocking collectives: 9.78 us -> 11.1 us  [body(): glogk = lax.all_to_all(glogk, 'modes', 0, 0)]
    ppermute x2, starting transfers between devices: 0.63 us -> 1.8 us  [exchange(): return lax.ppermute(value, AXES, [(i, i ^ mask) for i in range(size)])]
    ppermute x2, waiting for transfers between devices: 6.52 us -> 5.34 us  [exchange(): return lax.ppermute(value, AXES, [(i, i ^ mask) for i in range(size)])]
where the time goes in v4:
time: 82 us; the launch traced here: 81.7 us
  blocking collectives  45.4 us (55%)
  waiting for transfers between devices  15.5 us (19%)
  Pallas kernels  12 us (15%)
  starting transfers between devices  6.55 us (8%)
    all_to_all x1, blocking collectives, body(): pieces = lax.all_to_all(pieces, AXES, 0, 0, axis_index_groups=groups)  22.2 us
    all_to_all x1, blocking collectives, body(): parts = lax.all_to_all(partial_field, 'modes', 0, 0)  12.1 us
    all_to_all x1, blocking collectives, body(): glogk = lax.all_to_all(glogk, 'modes', 0, 0)  11.1 us
    all_to_all x1, waiting for transfers between devices, body(): grad_rows = lax.all_to_all(grad_rows, AXES, 0, 0, axis_index_groups=groups)  10.2 us
    pallas_call x1, Pallas kernels, physics(): pl.pallas_call(physics_kernel, in_specs=[VMEM] * 2, out_specs=[VMEM, VMEM...  8.41 us
    ppermute x2, waiting for transfers between devices, exchange(): return lax.ppermute(value, AXES, [(i, i ^ mask) for i in range(size)])  5.34 us
    all_to_all x1, starting transfers between devices, body(): grad_rows = lax.all_to_all(grad_rows, AXES, 0, 0, axis_index_groups=groups)  4.75 us
    pallas_call x1, Pallas kernels, field_of(): pl.pallas_call(field_kernel, in_specs=[pl.BlockSpec(memory_space=pltpu.HB...  2.24 us
  transfers between devices with their start and end apart: 3, of which 3 were waited for; matrix products, arithmetic and copies ran while one was open for 1% of the time, Pallas kernels for 0%

profile of v4, /device:TPU:8, one launch (start us, length us, event | category | flops | bytes accessed | tf_op | source)
XLA Modules:
  0.0 81.7 jit_solution(8928823117199606285)
XLA Ops:
  0.6 0.0 copy-start.8
  0.6 0.0 copy-start.7
  0.7 0.0 copy-start.6
  0.7 0.0 copy-start.5
  0.7 0.0 copy-start.4
  0.7 0.0 copy-start.3
  0.7 2.2 %field.1 = f32[32,16,128]{2,1,0:T(8,128)S(1)} custom-call(f32[32,512]{1,0:T(8,128)} %bitcast.24, bf16[2048,512]{1,0:T(8,128)(2,1)} %basis_ref.1), custom_call_target="tpu_custom_call" | custom-call | flops 67108864 | bytes 2097152 | tf_op jit(solution)/shard_map/field/pallas_call | solution.py:81
  3.0 12.1 %all_to_all.20.parts_ref = f32[16,2,16,128]{3,2,1,0:T(8,128)S(1)} all-to-all(f32[16,2,16,128]{3,2,1,0:T(8,128)S(1)} %bitcast.15), channel_id=1, replica_groups=mesh['cells'=16,'modes'=16] {'modes'}, dimensions={0} | all-to-all | bytes 524288 | tf_op jit(solution)/shard_map/all_to_all | solution.py:602
  15.0 0.0 copy-done.6
  15.0 0.0 copy-done.5
  15.1 0.0 copy-done.4
  15.1 0.0 copy-done.3
  15.1 0.0 copy-done.1
  15.1 0.0 copy-done.2
  15.1 0.2 combine.1
  15.3 22.2 %all_to_all.21.own_ref = s32[16,48,128]{2,1,0:T(8,128)S(1)} all-to-all(s32[16,48,128]{2,1,0:T(8,128)S(1)} %combine.1), channel_id=1, replica_groups={{0,16,32,48,64,80,96,112,128,144,160,176,192,208,224,240},{65,81,97,113..., dimensions={0} | all-to-all | bytes 786432 | tf_op jit(solution)/shard_map/all_to_all | solution.py:617
  37.5 0.0 collective-permute-start
  37.6 1.7 %collective-permute-done.other_ref = s32[16,48,128]{2,1,0:T(8,128)S(1)} collective-permute-done((s32[16,48,128]{2,1,0:T(8,128)S(1)}, s32[16,48,128]{2,1,0:T(8,128)S(1)}, u32[]{:S(2)}, u32[]{:S(2)}) %collective-permute-start) | collective-permute-done | bytes 393248 | tf_op jit(solution)/shard_map/ppermute | solution.py:582
  39.3 8.4 %physics.1 = (f32[2,16,128]{2,1,0:T(8,128)S(1)}, bf16[16,2,16,128]{3,2,1,0:T(8,128)(2,1)S(1)}) custom-call(s32[16,48,128]{2,1,0:T(8,128)S(1)} %all_to_all.21.own_ref, s32[16,48,128]{2,1,0:T(8,128)S(1)} %collective-permute-done.other_ref), custom_call_target="tpu_custom_call" | custom-call | flops 4294967296 | bytes 16777216 | tf_op jit(solution)/shard_map/physics/pallas_call | solution.py:505
  47.7 0.0 copy-start.9
  47.7 0.0 copy-start.11
  47.7 11.1 %all_to_all.22.glogk_ref = bf16[16,2,16,128]{3,2,1,0:T(8,128)(2,1)S(1)} all-to-all(bf16[16,2,16,128]{3,2,1,0:T(8,128)(2,1)S(1)} %get-tuple-element.5), channel_id=1, replica_groups=mesh['cells'=16,'modes'=16] {'modes'}, dimensions={0} | all-to-all | bytes 262144 | tf_op jit(solution)/shard_map/all_to_all | solution.py:620
  58.9 0.4 gradient.1.one_ref
  59.3 1.8 %collective-permute-start.1 = (bf16[32,512]{1,0:T(8,128)(2,1)S(1)}, bf16[32,512]{1,0:T(8,128)(2,1)S(1)}, u32[]{:S(2)}, u32[]{:S(2)}) collective-permute-start(bf16[32,512]{1,0:T(8,128)(2,1)S(1)} %gradient.1.one_ref), channel_id=1, source_target_pairs={{0,128},{1,129},{2,130},{3,131},{4,132},{5,133},{6,134},{7,135},{8... | collective-permute-start | bytes 98312 | tf_op jit(solution)/shard_map/ppermute | solution.py:582
  61.1 3.6 %collective-permute-done.1.two_ref = bf16[32,512]{1,0:T(8,128)(2,1)S(1)} collective-permute-done((bf16[32,512]{1,0:T(8,128)(2,1)S(1)}, bf16[32,512]{1,0:T(8,128)(2,1)S(1)}, u32[]{:S(2)}, u32[]{:S(2)}) %collective-permute-start.1) | collective-permute-done | bytes 32800 | tf_op jit(solution)/shard_map/ppermute | solution.py:582
  64.7 0.7 copies.1
  65.4 4.7 %all-to-all-start.3 = ((bf16[8,32,512]{2,1,0:T(8,128)(2,1)}), bf16[8,32,512]{2,1,0:T(8,128)(2,1)S(1)}, u32[]{:S(2)}, u32[]{:S(2)}) async-start(bf16[8,32,512]{2,1,0:T(8,128)(2,1)} %copies.1), calls=%async_computation.3 | async-start | bytes 524288 | tf_op jit(solution)/shard_map/all_to_all | solution.py:629
  70.2 0.6 copy.16
  70.8 10.2 %all-to-all-done.3 = bf16[8,32,512]{2,1,0:T(8,128)(2,1)S(1)} async-done(((bf16[8,32,512]{2,1,0:T(8,128)(2,1)}), bf16[8,32,512]{2,1,0:T(8,128)(2,1)S(1)}, u32[]{:S(2)}, u32[]{:S(2)}) %all-to-all-start.3) | async-done | bytes 262176 | tf_op jit(solution)/shard_map/all_to_all | solution.py:629
  81.0 0.0 copy-start.10
  81.0 0.7 multiply_add_fusion
  81.7 0.0 copy-done.10
  (9 shorter events, 0.1 us)
Async XLA Ops:
  0.6 14.4 %copy-start.8 = (f32[256]{0:T(256)S(1)}, f32[256]{0:T(256)}, u32[]{:S(2)}) copy-start(f32[256]{0:T(256)} %param.20) | copy-start | bytes 3076
  0.6 14.4 %copy-start.7 = (s32[256,2]{0,1:T(2,128)S(1)}, s32[256,2]{0,1:T(2,128)}, u32[]{:S(2)}) copy-start(s32[256,2]{0,1:T(2,128)} %param.19) | copy-start | bytes 6148
  0.7 14.4 %copy-start.6 = (f32[2048]{0:T(1024)S(1)}, f32[2048]{0:T(1024)}, u32[]{:S(2)}) copy-start(f32[2048]{0:T(1024)} %param.18) | copy-start | bytes 24580
  0.7 14.4 %copy-start.5 = (f32[2048]{0:T(1024)S(1)}, f32[2048]{0:T(1024)}, u32[]{:S(2)}) copy-start(f32[2048]{0:T(1024)} %param.17) | copy-start | bytes 24580
  0.7 14.4 %copy-start.4 = (f32[2048]{0:T(1024)S(1)}, f32[2048]{0:T(1024)}, u32[]{:S(2)}) copy-start(f32[2048]{0:T(1024)} %param.16) | copy-start | bytes 24580
  0.7 14.4 %copy-start.3 = (f32[2048]{0:T(1024)S(1)}, f32[2048]{0:T(1024)}, u32[]{:S(2)}) copy-start(f32[2048]{0:T(1024)} %param.15) | copy-start | bytes 24580
  0.7 14.4 %copy-start.1 = (f32[3,2048]{1,0:T(4,128)S(1)}, f32[3,2048]{1,0:T(4,128)}, u32[]{:S(2)}) copy-start(f32[3,2048]{1,0:T(4,128)} %face_ref.1) | copy-start | bytes 73732
  0.7 14.4 %copy-start.2 = (f32[2048]{0:T(1024)S(1)}, f32[2048]{0:T(1024)}, u32[]{:S(2)}) copy-start(f32[2048]{0:T(1024)} %param.13) | copy-start | bytes 24580
  37.5 21.3 %copy-start = (bf16[2048,512]{1,0:T(8,128)(2,1)S(1)}, bf16[2048,512]{1,0:T(8,128)(2,1)}, u32[]{:S(2)}) copy-start(bf16[2048,512]{1,0:T(8,128)(2,1)} %basis_ref.1) | copy-start | bytes 6291460
  37.5 1.7 %collective-permute-start = (s32[16,48,128]{2,1,0:T(8,128)S(1)}, s32[16,48,128]{2,1,0:T(8,128)S(1)}, u32[]{:S(2)}, u32[]{:S(2)}) collective-permute-start(s32[16,48,128]{2,1,0:T(8,128)S(1)} %all_to_all.21.own_ref), channel_id=1, source_target_pairs={{0,1},{1,0},{2,3},{3,2},{4,5},{5,4},{6,7},{7,6},{8,9},{9,8},{10,11... | collective-permute-start | bytes 1179656 | tf_op jit(solution)/shard_map/ppermute | solution.py:582
  47.7 33.3 %copy-start.9 = (f32[512,32]{0,1:T(8,128)S(1)}, f32[512,32]{0,1:T(8,128)}, u32[]{:S(2)}) copy-start(f32[512,32]{0,1:T(8,128)} %param.11) | copy-start | bytes 196612
  47.7 33.3 %copy-start.11 = (f32[512,32]{0,1:T(8,128)S(1)}, f32[512,32]{0,1:T(8,128)}, u32[]{:S(2)}) copy-start(f32[512,32]{0,1:T(8,128)} %param.21) | copy-start | bytes 196612
  59.3 5.4 %collective-permute-start.1 = (bf16[32,512]{1,0:T(8,128)(2,1)S(1)}, bf16[32,512]{1,0:T(8,128)(2,1)S(1)}, u32[]{:S(2)}, u32[]{:S(2)}) collective-permute-start(bf16[32,512]{1,0:T(8,128)(2,1)S(1)} %gradient.1.one_ref), channel_id=1, source_target_pairs={{0,128},{1,129},{2,130},{3,131},{4,132},{5,133},{6,134},{7,135},{8... | collective-permute-start | bytes 98312 | tf_op jit(solution)/shard_map/ppermute | solution.py:582
  65.4 15.5 %all-to-all-start.3 = ((bf16[8,32,512]{2,1,0:T(8,128)(2,1)}), bf16[8,32,512]{2,1,0:T(8,128)(2,1)S(1)}, u32[]{:S(2)}, u32[]{:S(2)}) async-start(bf16[8,32,512]{2,1,0:T(8,128)(2,1)} %copies.1), calls=%async_computation.3 | async-start | bytes 524288 | tf_op jit(solution)/shard_map/all_to_all | solution.py:629
  81.0 0.7 copy-start.10

commit v5 on v4

--- a/solution.py
+++ b/solution.py
@@ -29,7 +29,7 @@
 
 
 def turn(mode):
-    return 4 * (mode & 1) + 2 * (mode >> 1)
+    return mode
 
 
 def cost(flops, bytes_accessed):

time: 82 us -> 82.8 us (level)
  starting transfers between devices: 6.55 us -> 5.04 us
  blocking collectives: 45.4 us -> 46.7 us
  waiting for transfers between devices: 15.5 us -> 16.4 us
    all_to_all x1, blocking collectives: 22.2 us -> 24.7 us  [body(): pieces = lax.all_to_all(pieces, AXES, 0, 0, axis_index_groups=groups)]
    all_to_all x1, blocking collectives: 11.1 us -> 9.94 us  [body(): glogk = lax.all_to_all(glogk, 'modes', 0, 0)]
    all_to_all x1, starting transfers between devices: 4.75 us -> 3.87 us  [body(): grad_rows = lax.all_to_all(grad_rows, AXES, 0, 0, axis_index_groups=groups)]
where the time goes in v5:
time: 82.8 us; the launch traced here: 82.3 us
  blocking collectives  46.7 us (56%)
  waiting for transfers between devices  16.4 us (20%)
  Pallas kernels  12 us (14%)
  starting transfers between devices  5.04 us (6%)
    all_to_all x1, blocking collectives, body(): pieces = lax.all_to_all(pieces, AXES, 0, 0, axis_index_groups=groups)  24.7 us
    all_to_all x1, blocking collectives, body(): parts = lax.all_to_all(partial_field, 'modes', 0, 0)  12.1 us
    all_to_all x1, waiting for transfers between devices, body(): grad_rows = lax.all_to_all(grad_rows, AXES, 0, 0, axis_index_groups=groups)  10.4 us
    all_to_all x1, blocking collectives, body(): glogk = lax.all_to_all(glogk, 'modes', 0, 0)  9.94 us
    pallas_call x1, Pallas kernels, physics(): pl.pallas_call(physics_kernel, in_specs=[VMEM] * 2, out_specs=[VMEM, VMEM...  8.43 us
    ppermute x2, waiting for transfers between devices, exchange(): return lax.ppermute(value, AXES, [(i, i ^ mask) for i in range(size)])  5.98 us
    all_to_all x1, starting transfers between devices, body(): grad_rows = lax.all_to_all(grad_rows, AXES, 0, 0, axis_index_groups=groups)  3.87 us
    pallas_call x1, Pallas kernels, field_of(): pl.pallas_call(field_kernel, in_specs=[pl.BlockSpec(memory_space=pltpu.HB...  2.24 us
  transfers between devices with their start and end apart: 3, of which 3 were waited for; matrix products, arithmetic and copies ran while one was open for 1% of the time, Pallas kernels for 0%

profile of v5, /device:TPU:8, one launch (start us, length us, event | category | flops | bytes accessed | tf_op | source)
XLA Modules:
  0.0 82.3 jit_solution(1586784454767286644)
XLA Ops:
  0.6 0.0 copy-start.8
  0.6 0.0 copy-start.7
  0.7 0.0 copy-start.6
  0.7 0.0 copy-start.5
  0.7 2.2 %field.1 = f32[32,16,128]{2,1,0:T(8,128)S(1)} custom-call(f32[32,512]{1,0:T(8,128)} %bitcast.24, bf16[2048,512]{1,0:T(8,128)(2,1)} %basis_ref.1), custom_call_target="tpu_custom_call" | custom-call | flops 67108864 | bytes 2097152 | tf_op jit(solution)/shard_map/field/pallas_call | solution.py:81
  3.0 12.1 %all_to_all.20.parts_ref = f32[16,2,16,128]{3,2,1,0:T(8,128)S(1)} all-to-all(f32[16,2,16,128]{3,2,1,0:T(8,128)S(1)} %bitcast.15), channel_id=1, replica_groups=mesh['cells'=16,'modes'=16] {'modes'}, dimensions={0} | all-to-all | bytes 524288 | tf_op jit(solution)/shard_map/all_to_all | solution.py:602
  15.0 0.0 copy-done.6
  15.0 0.0 copy-done.5
  15.1 0.0 copy-done.4
  15.1 0.0 copy-done.3
  15.1 0.0 copy-done.1
  15.1 0.0 copy-done.2
  15.1 0.2 combine.1
  15.3 24.7 %all_to_all.21.own_ref = s32[16,48,128]{2,1,0:T(8,128)S(1)} all-to-all(s32[16,48,128]{2,1,0:T(8,128)S(1)} %combine.1), channel_id=1, replica_groups={{0,16,32,48,64,80,96,112,128,144,160,176,192,208,224,240},{17,33,49,65,..., dimensions={0} | all-to-all | bytes 786432 | tf_op jit(solution)/shard_map/all_to_all | solution.py:617
  40.0 0.0 collective-permute-start
  40.0 1.7 %collective-permute-done.other_ref = s32[16,48,128]{2,1,0:T(8,128)S(1)} collective-permute-done((s32[16,48,128]{2,1,0:T(8,128)S(1)}, s32[16,48,128]{2,1,0:T(8,128)S(1)}, u32[]{:S(2)}, u32[]{:S(2)}) %collective-permute-start) | collective-permute-done | bytes 393248 | tf_op jit(solution)/shard_map/ppermute | solution.py:582
  41.7 8.4 %physics.1 = (f32[2,16,128]{2,1,0:T(8,128)S(1)}, bf16[16,2,16,128]{3,2,1,0:T(8,128)(2,1)S(1)}) custom-call(s32[16,48,128]{2,1,0:T(8,128)S(1)} %all_to_all.21.own_ref, s32[16,48,128]{2,1,0:T(8,128)S(1)} %collective-permute-done.other_ref), custom_call_target="tpu_custom_call" | custom-call | flops 4294967296 | bytes 16777216 | tf_op jit(solution)/shard_map/physics/pallas_call | solution.py:505
  50.2 0.0 copy-start.9
  50.2 0.0 copy-start.11
  50.2 9.9 %all_to_all.22.glogk_ref = bf16[16,2,16,128]{3,2,1,0:T(8,128)(2,1)S(1)} all-to-all(bf16[16,2,16,128]{3,2,1,0:T(8,128)(2,1)S(1)} %get-tuple-element.5), channel_id=1, replica_groups=mesh['cells'=16,'modes'=16] {'modes'}, dimensions={0} | all-to-all | bytes 262144 | tf_op jit(solution)/shard_map/all_to_all | solution.py:620
  60.1 0.0 copy-done
  60.1 0.4 gradient.1.one_ref
  60.6 1.2 %collective-permute-start.1 = (bf16[32,512]{1,0:T(8,128)(2,1)S(1)}, bf16[32,512]{1,0:T(8,128)(2,1)S(1)}, u32[]{:S(2)}, u32[]{:S(2)}) collective-permute-start(bf16[32,512]{1,0:T(8,128)(2,1)S(1)} %gradient.1.one_ref), channel_id=1, source_target_pairs={{0,128},{1,129},{2,130},{3,131},{4,132},{5,133},{6,134},{7,135},{8... | collective-permute-start | bytes 98312 | tf_op jit(solution)/shard_map/ppermute | solution.py:582
  61.7 4.3 %collective-permute-done.1.two_ref = bf16[32,512]{1,0:T(8,128)(2,1)S(1)} collective-permute-done((bf16[32,512]{1,0:T(8,128)(2,1)S(1)}, bf16[32,512]{1,0:T(8,128)(2,1)S(1)}, u32[]{:S(2)}, u32[]{:S(2)}) %collective-permute-start.1) | collective-permute-done | bytes 32800 | tf_op jit(solution)/shard_map/ppermute | solution.py:582
  66.0 0.7 copies.1
  66.7 3.9 %all-to-all-start.3 = ((bf16[8,32,512]{2,1,0:T(8,128)(2,1)}), bf16[8,32,512]{2,1,0:T(8,128)(2,1)S(1)}, u32[]{:S(2)}, u32[]{:S(2)}) async-start(bf16[8,32,512]{2,1,0:T(8,128)(2,1)} %copies.1), calls=%async_computation.3 | async-start | bytes 524288 | tf_op jit(solution)/shard_map/all_to_all | solution.py:629
  70.6 0.6 copy.16
  71.2 10.4 %all-to-all-done.3 = bf16[8,32,512]{2,1,0:T(8,128)(2,1)S(1)} async-done(((bf16[8,32,512]{2,1,0:T(8,128)(2,1)}), bf16[8,32,512]{2,1,0:T(8,128)(2,1)S(1)}, u32[]{:S(2)}, u32[]{:S(2)}) %all-to-all-start.3) | async-done | bytes 262176 | tf_op jit(solution)/shard_map/all_to_all | solution.py:629
  81.6 0.0 copy-done.9
  81.6 0.0 copy-done.11
  81.6 0.0 copy-start.10
  81.7 0.7 multiply_add_fusion
  (9 shorter events, 0.1 us)
Async XLA Ops:
  0.6 14.4 %copy-start.8 = (f32[256]{0:T(256)S(1)}, f32[256]{0:T(256)}, u32[]{:S(2)}) copy-start(f32[256]{0:T(256)} %param.20) | copy-start | bytes 3076
  0.6 14.4 %copy-start.7 = (s32[256,2]{0,1:T(2,128)S(1)}, s32[256,2]{0,1:T(2,128)}, u32[]{:S(2)}) copy-start(s32[256,2]{0,1:T(2,128)} %param.19) | copy-start | bytes 6148
  0.7 14.4 %copy-start.6 = (f32[2048]{0:T(1024)S(1)}, f32[2048]{0:T(1024)}, u32[]{:S(2)}) copy-start(f32[2048]{0:T(1024)} %param.18) | copy-start | bytes 24580
  0.7 14.4 %copy-start.5 = (f32[2048]{0:T(1024)S(1)}, f32[2048]{0:T(1024)}, u32[]{:S(2)}) copy-start(f32[2048]{0:T(1024)} %param.17) | copy-start | bytes 24580
  0.7 14.4 %copy-start.4 = (f32[2048]{0:T(1024)S(1)}, f32[2048]{0:T(1024)}, u32[]{:S(2)}) copy-start(f32[2048]{0:T(1024)} %param.16) | copy-start | bytes 24580
  0.7 14.4 %copy-start.3 = (f32[2048]{0:T(1024)S(1)}, f32[2048]{0:T(1024)}, u32[]{:S(2)}) copy-start(f32[2048]{0:T(1024)} %param.15) | copy-start | bytes 24580
  0.7 14.4 %copy-start.1 = (f32[3,2048]{1,0:T(4,128)S(1)}, f32[3,2048]{1,0:T(4,128)}, u32[]{:S(2)}) copy-start(f32[3,2048]{1,0:T(4,128)} %face_ref.1) | copy-start | bytes 73732
  0.7 14.4 %copy-start.2 = (f32[2048]{0:T(1024)S(1)}, f32[2048]{0:T(1024)}, u32[]{:S(2)}) copy-start(f32[2048]{0:T(1024)} %param.13) | copy-start | bytes 24580
  40.0 20.1 %copy-start = (bf16[2048,512]{1,0:T(8,128)(2,1)S(1)}, bf16[2048,512]{1,0:T(8,128)(2,1)}, u32[]{:S(2)}) copy-start(bf16[2048,512]{1,0:T(8,128)(2,1)} %basis_ref.1) | copy-start | bytes 6291460
  40.0 1.7 %collective-permute-start = (s32[16,48,128]{2,1,0:T(8,128)S(1)}, s32[16,48,128]{2,1,0:T(8,128)S(1)}, u32[]{:S(2)}, u32[]{:S(2)}) collective-permute-start(s32[16,48,128]{2,1,0:T(8,128)S(1)} %all_to_all.21.own_ref), channel_id=1, source_target_pairs={{0,1},{1,0},{2,3},{3,2},{4,5},{5,4},{6,7},{7,6},{8,9},{9,8},{10,11... | collective-permute-start | bytes 1179656 | tf_op jit(solution)/shard_map/ppermute | solution.py:582
  50.2 31.4 %copy-start.9 = (f32[512,32]{0,1:T(8,128)S(1)}, f32[512,32]{0,1:T(8,128)}, u32[]{:S(2)}) copy-start(f32[512,32]{0,1:T(8,128)} %param.11) | copy-start | bytes 196612
  50.2 31.4 %copy-start.11 = (f32[512,32]{0,1:T(8,128)S(1)}, f32[512,32]{0,1:T(8,128)}, u32[]{:S(2)}) copy-start(f32[512,32]{0,1:T(8,128)} %param.21) | copy-start | bytes 196612
  60.6 5.4 %collective-permute-start.1 = (bf16[32,512]{1,0:T(8,128)(2,1)S(1)}, bf16[32,512]{1,0:T(8,128)(2,1)S(1)}, u32[]{:S(2)}, u32[]{:S(2)}) collective-permute-start(bf16[32,512]{1,0:T(8,128)(2,1)S(1)} %gradient.1.one_ref), channel_id=1, source_target_pairs={{0,128},{1,129},{2,130},{3,131},{4,132},{5,133},{6,134},{7,135},{8... | collective-permute-start | bytes 98312 | tf_op jit(solution)/shard_map/ppermute | solution.py:582
  66.7 14.9 %all-to-all-start.3 = ((bf16[8,32,512]{2,1,0:T(8,128)(2,1)}), bf16[8,32,512]{2,1,0:T(8,128)(2,1)S(1)}, u32[]{:S(2)}, u32[]{:S(2)}) async-start(bf16[8,32,512]{2,1,0:T(8,128)(2,1)} %copies.1), calls=%async_computation.3 | async-start | bytes 524288 | tf_op jit(solution)/shard_map/all_to_all | solution.py:629
  81.6 0.7 copy-start.10
